TPU v7x, 512 devices: a whole 4x8x8 slice. The times are simulated.
512 devices in a mesh: row: 16 (over y, core), col: 32 (over x, z).
Axes of the slice: x: 4, y: 8, z: 8, core: 2. Of those that a mesh axis runs over, the one named last changes fastest.
Arguments:
- momentum: bfloat16 [8192, 36864], P('row', 'col'), may hold values from -6 to 6
- gradient: bfloat16 [8192, 36864], P('row', 'col'), may hold values from -250 to 250
- right_factor: float32 [36864, 256], P(('col', 'row')), may hold values from -0.03125 to 0.03125
Outputs:
- new_momentum: bfloat16 [8192, 36864], P('row', 'col')
- step_update: bfloat16 [8192, 36864], P('row', 'col')
- new_right_factor: float32 [36864, 256], P(('col', 'row'))
All inputs are finite; a program needn't handle non-finite values.
Results may differ from a plain program's by a relative error of at most 0.012.
Values may be sent and summed in bfloat16 or wider, within the bound.
A program may use at most 64 MiB of HBM per device.

v0:
```python
import math

import jax
import jax.numpy as jnp
from jax import lax
from jax.sharding import PartitionSpec as P


def gram_from(panel_rows):
    return lax.dot_general(
        panel_rows, panel_rows, (((0,), (0,)), ((), ())), precision=lax.Precision.HIGHEST
    )


def orthonormal(panel_rows, gram_matrix):
    lower = jnp.linalg.cholesky(gram_matrix)
    solved = lax.linalg.triangular_solve(
        lower, panel_rows, left_side=False, lower=True, transpose_a=True
    )
    return solved.astype(jnp.bfloat16)


def outer_rows(left_basis, right_rows):
    return lax.dot_general(
        left_basis, right_rows, (((1,), (1,)), ((), ())), preferred_element_type=jnp.float32
    )


def body(momentum, gradient, right_factor):
    buffer = (momentum.astype(jnp.float32) + gradient.astype(jnp.float32)).astype(jnp.bfloat16)
    factor_low = right_factor.astype(jnp.bfloat16)
    rows_dev = buffer.shape[0]
    cols_dev = buffer.shape[1]
    rank_width = right_factor.shape[1]
    update_scale = math.sqrt(
        rows_dev * lax.axis_size("row") * cols_dev * lax.axis_size("col") / rank_width
    )
    partial_panel = jnp.dot(
        buffer,
        lax.all_gather(factor_low, "row", axis=0, tiled=True),
        preferred_element_type=jnp.float32,
    )
    left_panel = lax.psum(partial_panel, "col")
    gram_matrix = lax.psum(gram_from(left_panel), "row")
    left_basis = orthonormal(left_panel, gram_matrix)
    partial_coeff = lax.dot_general(
        buffer, left_basis, (((0,), (0,)), ((), ())), preferred_element_type=jnp.float32
    )
    coefficients = lax.psum(partial_coeff, "row")
    column_norms = lax.psum(jnp.sum(coefficients * coefficients, axis=0), "col")
    inverse = 1.0 / jnp.sqrt(column_norms + 1e-06)
    whole_factor = coefficients * inverse
    correction = outer_rows(left_basis, coefficients.astype(jnp.bfloat16))
    direction = outer_rows(left_basis, whole_factor.astype(jnp.bfloat16))
    amount = cols_dev // lax.axis_size("row")
    new_right_factor = lax.dynamic_slice_in_dim(
        whole_factor, lax.axis_index("row") * amount, amount, 0
    )
    new_momentum = (buffer.astype(jnp.float32) - 0.05 * correction).astype(jnp.bfloat16)
    step_update = (update_scale * direction).astype(jnp.bfloat16)
    return (new_momentum, step_update, new_right_factor)


def solution(mesh):
    placed = (P("row", "col"), P("row", "col"), P(("col", "row"), None))
    return jax.shard_map(
        body,
        mesh=mesh,
        in_specs=placed,
        out_specs=(P("row", "col"), P("row", "col"), P(("col", "row"), None)),
        check_vma=False,
    )
```

profile of v0, /device:TPU:32, one launch (start us, length us, event | category | flops | bytes accessed | tf_op | source)
XLA Modules:
  0.0 576.3 jit_solution(1588217562926603526)
XLA Ops:
  7.2 0.9 convert_element_type.32
  8.1 16.6 %all_gather.3 = bf16[1152,256]{1,0:T(8,128)(2,1)S(1)} all-gather(bf16[72,256]{1,0:T(8,128)(2,1)S(1)} %convert_element_type.32), channel_id=1, replica_groups=mesh['row'=16,'col'=32] {'row'}, dimensions={0}, use_global_device_ids=true | all-gather | bytes 626688 | tf_op jit(solution)/shard_map/all_gather | solution.py:40
  24.7 2.9 fusion.16
  27.7 163.3 %all-reduce.5.cloned.1.call-done = f32[512,256]{1,0:T(8,128)} async-done(((f32[512,256]{1,0:T(8,128)}), f32[512,256]{1,0:T(8,128)}) %all-reduce.5.cloned.1.call-update) | async-done | bytes 524304 | tf_op jit(solution)/shard_map/psum | solution.py:43
  191.0 2.9 fusion.19
  194.0 110.0 %all-reduce.7.cloned.1.call-done = f32[256,256]{0,1:T(8,128)} async-done(((f32[256,256]{0,1:T(8,128)}), f32[256,256]{0,1:T(8,128)}) %all-reduce.7.cloned.1.call-update) | async-done | bytes 262160 | tf_op jit(solution)/shard_map/psum | solution.py:44
  304.0 1.1 copy.7
  305.1 1.0 fusion.7
  306.1 11.7 %cholesky.50 = f32[128,128]{1,0:T(8,128)S(1)} custom-call(f32[128,128]{1,0:T(8,128)S(1)} %cholesky.118), custom_call_target="Cholesky" | custom-call | tf_op jit(solution)/shard_map/jit(cholesky)/cholesky | solution.py:16
  317.9 9.8 %custom-call.14 = f32[1,128,128]{1,2,0:T(8,128)S(1)} custom-call(f32[1,128,128]{2,1,0:T(8,128)S(1)} %get-tuple-element.24), custom_call_target="InvertDiagBlocksLowerTriangular" | custom-call | tf_op jit(solution)/shard_map/jit(cholesky)/cholesky | solution.py:16
  328.2 11.7 %cholesky.105 = f32[128,128]{1,0:T(8,128)S(1)} custom-call(f32[128,128]{1,0:T(8,128)S(1)} %convolution_subtract_fusion.1), custom_call_target="Cholesky" | custom-call | tf_op jit(solution)/shard_map/jit(cholesky)/cholesky | solution.py:16
  339.9 0.6 compare_reduce_fusion
  342.0 4.1 while.1
  342.7 1.4 bitcast_dynamic-update-slice_fusion.2
  344.7 1.4 bitcast_dynamic-update-slice_fusion.2
  346.1 19.7 %custom-call.15 = f32[2,128,128]{1,2,0:T(8,128)S(1)} custom-call(f32[2,128,128]{2,1,0:T(8,128)S(1)} %get-tuple-element.10), custom_call_target="InvertDiagBlocksLowerTriangular" | custom-call | tf_op jit(solution)/shard_map/triangular_solve | solution.py:17
  368.0 1.5 fusion.8
  369.5 118.1 %all-reduce.9.cloned.1.call-done = f32[1152,256]{1,0:T(8,128)} async-done(((f32[1152,256]{1,0:T(8,128)}), f32[1152,256]{1,0:T(8,128)}) %all-reduce.9.cloned.1.call-update) | async-done | bytes 1179664 | tf_op jit(solution)/shard_map/psum | solution.py:49
  487.7 1.5 multiply_reduce_fusion
  489.2 75.7 %psum.31 = f32[256]{0:T(256)S(1)} all-reduce(f32[256]{0:T(256)S(1)} %multiply_reduce_fusion), channel_id=1, replica_groups=mesh['row'=16,'col'=32] {'col'}, use_global_device_ids=true, to_apply=%region_8.9 | all-reduce | flops 256 | bytes 2048 | tf_op jit(solution)/shard_map/psum | solution.py:50
  565.0 0.8 copy-done.5
  565.9 1.6 fusion.2
  567.5 0.6 constant_dynamic-slice_fusion.1
  568.1 1.7 fusion.1
  (40 shorter events, 4.3 us)
Async XLA Ops:
  7.2 183.8 %all-reduce.5.cloned.1.call-start = ((), (), s32[]{:S(2)}) async-start(), calls=%async_computation | async-start | bytes 1048576 | tf_op jit(solution)/shard_map/psum | solution.py:43
  27.7 276.3 %all-reduce.7.cloned.1.call-start = ((), (), s32[]{:S(2)}) async-start(), calls=%async_computation.1 | async-start | bytes 524288 | tf_op jit(solution)/shard_map/psum | solution.py:44
  193.9 293.7 %all-reduce.9.cloned.1.call-start = ((), (), s32[]{:S(2)}) async-start(), calls=%async_computation.2 | async-start | bytes 2359296 | tf_op jit(solution)/shard_map/psum | solution.py:49
  317.9 48.0 %copy-start.3 = (f32[512,256]{1,0:T(8,128)S(1)}, f32[512,256]{1,0:T(8,128)}, u32[]{:S(2)}) copy-start(f32[512,256]{1,0:T(8,128)} %all-reduce.5.cloned.1.call-done) | copy-start | bytes 1572868
  341.9 26.1 %copy-start.2 = (bf16[512,1152]{1,0:T(8,128)(2,1)S(1)}, bf16[512,1152]{1,0:T(8,128)(2,1)}, u32[]{:S(2)}) copy-start(bf16[512,1152]{1,0:T(8,128)(2,1)} %param.3) | copy-start | bytes 3538948
  346.1 21.8 %copy-start.1 = (bf16[512,1152]{1,0:T(8,128)(2,1)S(1)}, bf16[512,1152]{1,0:T(8,128)(2,1)}, u32[]{:S(2)}) copy-start(bf16[512,1152]{1,0:T(8,128)(2,1)} %param.4) | copy-start | bytes 3538948
  366.3 1.1 copy-start.6
  367.3 0.7 copy-start.4
  487.7 77.2 %copy-start = (f32[1152,256]{1,0:T(8,128)S(1)}, f32[1152,256]{1,0:T(8,128)}, u32[]{:S(2)}) copy-start(f32[1152,256]{1,0:T(8,128)} %all-reduce.9.cloned.1.call-done) | copy-start | bytes 3538948
  564.9 0.9 copy-start.5
  564.9 1.0 copy-start.7
Sparse Core Ops, SparseCore 0:
  27.8 163.1 all-reduce.4
  194.0 109.9 all-reduce.6
  369.6 117.9 all-reduce.8
where the time goes:
time: 577 us; the launch traced here: 576 us
  waiting for transfers between devices  391 us (68%)
  blocking collectives  92.3 us (16%)
  other arithmetic  57.2 us (10%)
  between operations  15.2 us (3%)
  matrix products  12.5 us (2%)
  local copies, waits for them, and re-layouts  7.3 us (1%)
    psum x1, waiting for transfers between devices, body(): left_panel = lax.psum(partial_panel, 'col')  163 us
    psum x1, waiting for transfers between devices, body(): coefficients = lax.psum(partial_coeff, 'row')  118 us
    psum x1, waiting for transfers between devices, body(): gram_matrix = lax.psum(gram_from(left_panel), 'row')  110 us
    psum x1, blocking collectives, body(): column_norms = lax.psum(jnp.sum(coefficients * coefficients, axis=0), 'col')  75.7 us
    another operation x6, other arithmetic, orthonormal(): lower = jnp.linalg.cholesky(gram_matrix)  33.9 us
    another operation x3, other arithmetic, orthonormal(): lax.linalg.triangular_solve(lower, panel_rows, left_side=False, lower=Tru...  19.7 us
    all_gather x1, blocking collectives, body(): lax.all_gather(factor_low, 'row', axis=0, tiled=True)  16.6 us
  transfers between devices with their start and end apart: 3, of which 3 were waited for; matrix products, arithmetic and copies ran while one was open for 0% of the time, Pallas kernels for 0%

commit v1 on v0

v1 whole, which is shorter than its diff:
```python
import functools
import math

import jax
import jax.numpy as jnp
from jax import lax
from jax.experimental import pallas as pl
from jax.experimental.pallas import tpu as pltpu
from jax.sharding import PartitionSpec as P

MESH = pl.DeviceIdType.MESH
LANES = 128
X_CHIPS = 4
F32 = jnp.float32
BF16 = jnp.bfloat16


def dot(a, b):
    return jnp.dot(a, b, preferred_element_type=F32)


def dot_nt(a, b):
    return lax.dot_general(a, b, (((1,), (1,)), ((), ())), preferred_element_type=F32)


def split(value):
    high = value.astype(BF16)
    return high, (value - high.astype(F32)).astype(BF16)


def splat(rows, lane):
    return jnp.broadcast_to(rows[:, lane : lane + 1], (rows.shape[0], LANES))


def eliminate(block):
    n = LANES
    lanes = lax.broadcasted_iota(jnp.int32, (8, LANES), 1)
    sublane = lax.broadcasted_iota(jnp.int32, (8, LANES), 0)
    groups = [block[8 * g : 8 * g + 8, :] for g in range(n // 8)]
    for j in range(n // 8):
        base = 8 * j
        inside = (lanes >= base) & (lanes < base + 8)
        rows = [jnp.broadcast_to(groups[j][k : k + 1, :], (8, LANES)) for k in range(8)]
        entry = {(i, k): splat(rows[k], base + i) for k in range(8) for i in range(k, 8)}
        rows = [jnp.where(inside, jnp.where(lanes == base + k, 1.0, 0.0), rows[k]) for k in range(8)]
        low, inv = {}, {}
        for k in range(8):
            root = lax.rsqrt(entry[k, k])
            for i in range(k + 1, 8):
                low[i, k] = entry[i, k] * root
            for m in range(k + 1, 8):
                for i in range(m, 8):
                    entry[i, m] = entry[i, m] - low[i, k] * low[m, k]
            rows[k] = rows[k] * root
            for i in range(k + 1, 8):
                rows[i] = rows[i] - low[i, k] * rows[k]
            inv[k, k] = root
            for i in range(k):
                total = low[k, i] * inv[i, i]
                for m in range(i + 1, k):
                    total = total + low[k, m] * inv[m, i]
                inv[k, i] = -(total * root)
        value = rows[0]
        for k in range(1, 8):
            value = jnp.where(sublane == k, rows[k], value)
        groups[j] = value
        if j == n // 8 - 1:
            break
        back = []
        for i in range(8):
            terms = [inv[k, i] * rows[k] for k in range(i, 8)]
            while len(terms) > 1:
                terms = [sum(terms[a : a + 2][1:], terms[a]) for a in range(0, len(terms), 2)]
            back.append(terms[0])
        for g in range(j + 1, n // 8):
            columns = [splat(groups[g], base + k) for k in range(8)]
            terms = [columns[k] * back[k] for k in range(8)]
            while len(terms) > 1:
                terms = [terms[a] + terms[a + 1] for a in range(0, len(terms), 2)]
            groups[g] = jnp.where(inside, 0.0, groups[g]) - terms[0]
    whole = jnp.concatenate(groups, axis=0)
    at_row = lax.broadcasted_iota(jnp.int32, (n, n), 0)
    at_col = lax.broadcasted_iota(jnp.int32, (n, n), 1)
    return jnp.where(at_row >= at_col, whole, 0.0)


def exact(a, b, dims):
    return lax.dot_general(a, b, ((dims[:1], dims[1:]), ((), ())), precision=lax.Precision.HIGHEST)


def inverse_lower(work, out_ref, hook):
    top, rest = slice(0, LANES), slice(LANES, 2 * LANES)
    first = eliminate(work[top, top])
    out_ref[top, top] = first
    out_ref[top, rest] = jnp.zeros((LANES, LANES), F32)
    upper = exact(first, work[top, rest], (1, 0))
    schur = work[rest, rest] - exact(upper, upper, (0, 0))
    hook()
    second = eliminate(schur)
    out_ref[rest, rest] = second
    out_ref[rest, top] = -exact(second, exact(upper, first, (0, 0)), (1, 0))


def remote(src, dst, send, recv, device):
    return pltpu.make_async_remote_copy(
        src_ref=src, dst_ref=dst, send_sem=send, recv_sem=recv, device_id=device, device_id_type=MESH
    )


def step_kernel(
    sizes,
    momentum,
    gradient,
    factor,
    buf,
    basis_low,
    scaled_out,
    coeff_low,
    right_out,
    *scratch,
):
    ny, nx, nz, scale = sizes
    (
        grad, fown, fslot, fall, part, psend, xgot, zsend, zgot, panel, panel_t,
        gpart, ggot, gall, work, lower_inv, wpart, wsib, wsibgot, wsend, wgot, wall, coeff_t,
        nown, nxgot, nmid, nzgot,
        local_sem, f_send, f_recv, fs_send, fs_recv,
        x_send, x_recv, z_send, z_recv, pz_send, pz_recv, px_send, px_recv,
        gy_send, gy_recv, gz_send, gz_recv, gx_send, gx_recv, gs_send, gs_recv,
        ws_send, ws_recv, wy_send, wy_recv, wa_send, wa_recv, wf_send, wf_recv,
        nx_send, nx_recv, nz_send, nz_recv,
    ) = scratch
    row, col = lax.axis_index("row"), lax.axis_index("col")
    y, core = row // 2, row % 2
    x, z = col // nz, col % nz
    frows, rank = factor.shape
    rows_dev, cols_dev = buf.shape
    ncol = nx * nz
    sibling = (y * 2 + 1 - core, col)

    def at_y(d, flip=0):
        core_to = core if flip == 0 else 1 - core
        return (lax.rem(y + d, ny) * 2 + core_to, col)

    def at_x(d):
        return (row, lax.rem(x + d, nx) * nz + z)

    def at_z(d):
        return (row, x * nz + lax.rem(z + d, nz))

    started = []

    def send(copy):
        copy.start()
        started.append(copy)

    loads = [
        pltpu.make_async_copy(momentum, buf, local_sem.at[0]),
        pltpu.make_async_copy(gradient, grad, local_sem.at[1]),
        pltpu.make_async_copy(factor, fown, local_sem.at[2]),
    ]
    for copy in loads[::-1]:
        copy.start()

    peers = [at_y(d, flip) for d in range(ny) for flip in range(2) if (d, flip) != (0, 0)]
    peers += [at_x(d) for d in range(1, nx)] + [at_z(d) for d in range(1, nz)]
    barrier = pltpu.get_barrier_semaphore()
    for peer in peers:
        pl.semaphore_signal(barrier, inc=1, device_id=peer, device_id_type=MESH)
    loads[2].wait()
    fslot[row] = jnp.concatenate([fown[:, :LANES], fown[:, LANES:]], axis=0).astype(BF16)
    pl.semaphore_wait(barrier, len(peers))

    for d in sorted(range(1, ny), key=lambda d: -min(d, ny - d)):
        send(remote(fslot.at[row], fslot.at[row], f_send.at[d], f_recv.at[d], at_y(d)))
    send(remote(fslot.at[row], fslot.at[row], fs_send.at[0], fs_recv.at[0], sibling))
    loads[0].wait()
    loads[1].wait()

    def add_rows(i, carry):
        here = pl.ds(pl.multiple_of(i * 32, 32), 32)
        buf[here, :] = (buf[here, :].astype(F32) + grad[here, :].astype(F32)).astype(BF16)
        return carry

    lax.fori_loop(0, rows_dev // 32, add_rows, 0)

    def unpack(source):
        whole = fslot[source].astype(F32)
        here = pl.ds(pl.multiple_of(source * frows, 8), frows)
        fall[here, :LANES] = whole[:frows]
        fall[here, LANES:] = whole[frows:]

    unpack(row)
    near = sorted(range(1, ny), key=lambda d: min(d, ny - d))
    for d in near:
        source = lax.rem(y + ny - d, ny) * 2 + core
        remote(fslot.at[source], fslot.at[source], f_send.at[d], f_recv.at[d], at_y(ny - d)).wait_recv()
        send(remote(fslot.at[source], fslot.at[source], fs_send.at[d], fs_recv.at[d], sibling))
        unpack(source)
    for d in [0] + near:
        source = lax.rem(y + ny - d, ny) * 2 + 1 - core
        remote(fslot.at[source], fslot.at[source], fs_send.at[d], fs_recv.at[d], sibling).wait_recv()
        unpack(source)

    prow = rows_dev // ncol
    right = fall[...].astype(BF16)
    many = rows_dev // nx
    halves_z = [pl.ds(h * (nz // 2), nz // 2) for h in range(2)]
    for dx in list(range(1, nx)) + [0]:
        group = lax.rem(x + dx, nx)
        value = dot(buf[pl.ds(pl.multiple_of(group * many, many), many), :], right)
        if dx == 0:
            part[...] = value.reshape(nz, prow, rank)
            continue
        psend[dx] = value.astype(BF16).reshape(nz, prow, rank)
        for h in range(2):
            src, dst = psend.at[dx, halves_z[h]], xgot.at[dx, halves_z[h]]
            send(remote(src, dst, x_send.at[dx, h], x_recv.at[dx, h], at_x(dx)))
    for h in range(2):
        here = halves_z[h]
        value = part[here]
        for dx in range(1, nx):
            got = xgot.at[dx, here]
            remote(got, got, x_send.at[dx, h], x_recv.at[dx, h], at_x(dx)).wait_recv()
            value = value + xgot[dx, here].astype(F32)
        part[here] = value
        zsend[here] = value.astype(BF16)
        for i in range(nz // 2):
            to = h * (nz // 2) + i
            away = lax.rem(to - z + nz, nz)

            @pl.when(away != 0)
            def _(to=to, away=away):
                copy = remote(zsend.at[to], zgot.at[away], z_send.at[away], z_recv.at[away], (row, x * nz + to))
                copy.start()

    value = part[z]
    for dz in range(1, nz):
        remote(zgot.at[dz], zgot.at[dz], z_send.at[dz], z_recv.at[dz], at_z(dz)).wait_recv()
        value = value + zgot[dz].astype(F32)
    panel[col] = value.astype(BF16)
    for dz in sorted(range(1, nz), key=lambda d: -min(d, nz - d)):
        send(remote(panel.at[col], panel.at[col], pz_send.at[dz], pz_recv.at[dz], at_z(dz)))
    for step in range(2):
        lot = z // (nz // 2) if step == 0 else 1 - z // (nz // 2)
        for i in range(nz // 2):
            source = lot * (nz // 2) + i
            away = lax.rem(z - source + nz, nz)
            got = panel.at[x * nz + source]

            @pl.when(away != 0)
            def _(got=got, away=away):
                remote(got, got, pz_send.at[away], pz_recv.at[away], at_z(1)).wait_recv()

        group = panel.at[pl.ds(x * nz + lot * (nz // 2), nz // 2)]
        for dx in range(1, nx):
            send(remote(group, group, px_send.at[dx, step], px_recv.at[dx, step], at_x(dx)))
    for step in range(2):
        lot = z // (nz // 2) if step == 0 else 1 - z // (nz // 2)
        for dx in range(1, nx):
            group = panel.at[pl.ds(lax.rem(x + nx - dx, nx) * nz + lot * (nz // 2), nz // 2)]
            remote(group, group, px_send.at[dx, step], px_recv.at[dx, step], at_x(dx)).wait_recv()
    for dz in range(1, nz):
        got = zsend.at[lax.rem(z + dz, nz)]
        remote(got, got, z_send.at[dz], z_recv.at[dz], at_z(dz)).wait_send()

    left = panel[...].reshape(rows_dev, rank)
    left_t = left.T
    halves = rank // 2
    panel_t[...] = left_t.reshape(2, halves, rows_dev)
    grow = rank // ncol
    gram = dot(left_t, left)
    for h in range(2):
        gpart[h] = gram[:, h * LANES : (h + 1) * LANES].reshape(ncol, grow, LANES)
    gpeers = [(d, flip) for d in range(ny) for flip in range(2) if (d, flip) != (0, 0)]
    for d, flip in gpeers:
        half = core if flip == 0 else 1 - core
        send(remote(gpart.at[half, col], ggot.at[d, flip], gy_send.at[d, flip], gy_recv.at[d, flip], at_y(d, flip)))

    wrow = halves // ny
    value = dot(panel_t[1 - core], buf[...])
    wsib[...] = value.astype(BF16).reshape(ny, wrow, cols_dev)
    for d in list(range(1, ny)) + [0]:
        piece = lax.rem(y + d, ny)
        send(remote(wsib.at[piece], wsibgot.at[d], ws_send.at[d], ws_recv.at[d], sibling))
    value = dot(panel_t[core], buf[...])
    wpart[...] = value.reshape(ny, wrow, cols_dev)

    value = gpart[core, col]
    for d, flip in gpeers:
        remote(ggot.at[d, flip], ggot.at[d, flip], gy_send.at[d, flip], gy_recv.at[d, flip], at_y(d, flip)).wait_recv()
        value = value + ggot[d, flip]
    gall[core, col] = value
    for dz in range(1, nz):
        send(remote(gall.at[core, col], gall.at[core, col], gz_send.at[dz], gz_recv.at[dz], at_z(dz)))

    def merged(d):
        remote(wsibgot.at[d], wsibgot.at[d], ws_send.at[d], ws_recv.at[d], sibling).wait_recv()
        return wpart[lax.rem(y + d, ny)] + wsibgot[d].astype(F32)

    for d in sorted(range(1, ny), key=lambda d: -min(d, ny - d)):
        wsend[d] = merged(d).astype(BF16)
        send(remote(wsend.at[d], wgot.at[d], wy_send.at[d], wy_recv.at[d], at_y(d)))

    for dz in range(1, nz):
        got = gall.at[core, x * nz + lax.rem(z + nz - dz, nz)]
        remote(got, got, gz_send.at[dz], gz_recv.at[dz], at_z(dz)).wait_recv()
    group = gall.at[core, pl.ds(x * nz, nz)]
    for dx in range(1, nx):
        send(remote(group, group, gx_send.at[dx], gx_recv.at[dx], at_x(dx)))
    for dx in range(1, nx):
        group = gall.at[core, pl.ds(lax.rem(x + nx - dx, nx) * nz, nz)]
        remote(group, group, gx_send.at[dx], gx_recv.at[dx], at_x(dx)).wait_recv()
    send(remote(gall.at[core], gall.at[core], gs_send.at[0], gs_recv.at[0], sibling))
    remote(gall.at[1 - core], gall.at[1 - core], gs_send.at[0], gs_recv.at[0], sibling).wait_recv()
    for h in range(2):
        work[:, h * LANES : (h + 1) * LANES] = gall[h].reshape(rank, LANES)
    def finish_sum():
        value = merged(0)
        for d in range(1, ny):
            remote(wgot.at[d], wgot.at[d], wy_send.at[d], wy_recv.at[d], at_y(d)).wait_recv()
            value = value + wgot[d].astype(F32)
        mine = core * ny + y
        wall[mine] = value.astype(BF16)
        for d in sorted(range(1, ny), key=lambda d: -min(d, ny - d)):
            send(remote(wall.at[mine], wall.at[mine], wa_send.at[d], wa_recv.at[d], at_y(d)))
        send(remote(wall.at[mine], wall.at[mine], wf_send.at[0], wf_recv.at[0], sibling))

    def forward():
        for d in near:
            piece = core * ny + lax.rem(y + ny - d, ny)
            remote(wall.at[piece], wall.at[piece], wa_send.at[d], wa_recv.at[d], at_y(d)).wait_recv()
            send(remote(wall.at[piece], wall.at[piece], wf_send.at[d], wf_recv.at[d], sibling))

    inverse_lower(work, lower_inv, finish_sum)
    forward()
    high, low = split(lower_inv[...])
    basis = dot_nt(left, high) + dot_nt(left, low)
    basis_low[...] = basis.astype(BF16)
    for d in range(ny):
        piece = (1 - core) * ny + lax.rem(y + ny - d, ny)
        remote(wall.at[piece], wall.at[piece], wf_send.at[d], wf_recv.at[d], sibling).wait_recv()

    together = wall[...].reshape(rank, cols_dev)
    coeff_t[...] = dot(high, together) + dot(low, together)
    squares = jnp.zeros((rank, LANES), F32)
    for i in range(cols_dev // LANES):
        value = coeff_t[:, i * LANES : (i + 1) * LANES]
        squares = squares + value * value
    sums = squares.T
    value = sums[0:8]
    for i in range(1, LANES // 8):
        value = value + sums[8 * i : 8 * i + 8]
    nown[...] = value
    for dx in range(1, nx):
        send(remote(nown, nxgot.at[dx], nx_send.at[dx], nx_recv.at[dx], at_x(dx)))
    coeff_low[...] = coeff_t[...].astype(BF16)
    for dx in range(1, nx):
        remote(nxgot.at[dx], nxgot.at[dx], nx_send.at[dx], nx_recv.at[dx], at_x(dx)).wait_recv()
        value = value + nxgot[dx]
    nmid[...] = value
    for dz in range(1, nz):
        send(remote(nmid, nzgot.at[dz], nz_send.at[dz], nz_recv.at[dz], at_z(dz)))
    pick = lax.broadcasted_iota(jnp.int32, (frows, cols_dev), 1)
    pick = pick == lax.broadcasted_iota(jnp.int32, (frows, cols_dev), 0) + row * frows
    pick = jnp.where(pick, 1.0, 0.0).astype(BF16)
    c_high, c_low = split(coeff_t[...])
    mine = dot_nt(pick, c_high) + dot_nt(pick, c_low)
    for copy in started:
        copy.wait_send()
    for dz in range(1, nz):
        remote(nzgot.at[dz], nzgot.at[dz], nz_send.at[dz], nz_recv.at[dz], at_z(dz)).wait_recv()
        value = value + nzgot[dz]
    norms = jnp.sum(value, axis=0, keepdims=True)
    inverse = 1.0 / jnp.sqrt(norms + 1e-06)
    right_out[...] = mine * inverse
    scaled_out[...] = (basis * (inverse * scale)).astype(BF16)


def outputs_kernel(
    buffer, basis, scaled, coeff, right, momentum_out, update_out, right_out, momentum_low, update_low, sems, right_sem
):
    rows = momentum_low.shape[1]
    copies = [pltpu.make_async_copy(right, right_out, right_sem)]
    copies[0].start()
    for i in range(buffer.shape[0] // rows):
        here = slice(i * rows, (i + 1) * rows)
        update_low[i] = dot(scaled[here, :], coeff[...]).astype(BF16)
        copies.append(pltpu.make_async_copy(update_low.at[i], update_out.at[here], sems.at[0, i]))
        copies[-1].start()
        correction = dot(basis[here, :], coeff[...])
        momentum_low[i] = (buffer[here, :].astype(F32) - 0.05 * correction).astype(BF16)
        copies.append(pltpu.make_async_copy(momentum_low.at[i], momentum_out.at[here], sems.at[1, i]))
        copies[-1].start()
    for copy in copies:
        copy.wait()


def body(nx, momentum, gradient, right_factor):
    ny = lax.axis_size("row") // 2
    nz = lax.axis_size("col") // nx
    ncol = nx * nz
    rows_dev, cols_dev = momentum.shape
    frows, rank = right_factor.shape
    scale = math.sqrt(rows_dev * 2 * ny * cols_dev * ncol / rank)
    prow, grow, wrow = rows_dev // ncol, rank // ncol, rank // (2 * ny)
    sem = lambda *shape: pltpu.SemaphoreType.DMA(shape)
    scratch = [
        pltpu.VMEM((rows_dev, cols_dev), BF16),
        pltpu.VMEM((frows, rank), F32),
        pltpu.VMEM((2 * ny, 2 * frows, LANES), BF16),
        pltpu.VMEM((cols_dev, rank), F32),
        pltpu.VMEM((nz, prow, rank), F32),
        pltpu.VMEM((nx, nz, prow, rank), BF16),
        pltpu.VMEM((nx, nz, prow, rank), BF16),
        pltpu.VMEM((nz, prow, rank), BF16),
        pltpu.VMEM((nz, prow, rank), BF16),
        pltpu.VMEM((ncol, prow, rank), BF16),
        pltpu.VMEM((2, rank // 2, rows_dev), BF16),
        pltpu.VMEM((2, ncol, grow, LANES), F32),
        pltpu.VMEM((ny, 2, grow, LANES), F32),
        pltpu.VMEM((2, ncol, grow, LANES), F32),
        pltpu.VMEM((rank, rank), F32),
        pltpu.VMEM((rank, rank), F32),
        pltpu.VMEM((ny, wrow, cols_dev), F32),
        pltpu.VMEM((ny, wrow, cols_dev), BF16),
        pltpu.VMEM((ny, wrow, cols_dev), BF16),
        pltpu.VMEM((ny, wrow, cols_dev), BF16),
        pltpu.VMEM((ny, wrow, cols_dev), BF16),
        pltpu.VMEM((2 * ny, wrow, cols_dev), BF16),
        pltpu.VMEM((rank, cols_dev), F32),
        pltpu.VMEM((8, rank), F32),
        pltpu.VMEM((nx, 8, rank), F32),
        pltpu.VMEM((8, rank), F32),
        pltpu.VMEM((nz, 8, rank), F32),
        sem(3),
        sem(ny), sem(ny), sem(ny), sem(ny),
        sem(nx, 2), sem(nx, 2), sem(nz), sem(nz), sem(nz), sem(nz), sem(nx, 2), sem(nx, 2),
        sem(ny, 2), sem(ny, 2), sem(nz), sem(nz), sem(nx), sem(nx), sem(1), sem(1),
        sem(ny), sem(ny), sem(ny), sem(ny), sem(ny), sem(ny), sem(ny), sem(ny),
        sem(nx), sem(nx), sem(nz), sem(nz),
    ]
    momentum, gradient, right_factor = [
        pltpu.with_memory_space_constraint(value, pltpu.HBM) for value in (momentum, gradient, right_factor)
    ]
    whole = pl.BlockSpec(memory_space=pltpu.VMEM)
    hbm = pl.BlockSpec(memory_space=pltpu.HBM)
    buffer, basis, scaled, coeff, new_right = pl.pallas_call(
        functools.partial(step_kernel, (ny, nx, nz, scale)),
        out_shape=[
            jax.ShapeDtypeStruct((rows_dev, cols_dev), BF16),
            jax.ShapeDtypeStruct((rows_dev, rank), BF16),
            jax.ShapeDtypeStruct((rows_dev, rank), BF16),
            jax.ShapeDtypeStruct((rank, cols_dev), BF16),
            jax.ShapeDtypeStruct((frows, rank), F32),
        ],
        in_specs=[hbm] * 3,
        out_specs=[whole] * 5,
        scratch_shapes=scratch,
        compiler_params=pltpu.CompilerParams(
            collective_id=0, has_side_effects=True, vmem_limit_bytes=48 * 1024 * 1024
        ),
        name="panel_and_factor",
    )(momentum, gradient, right_factor)
    step = min(128, rows_dev)
    return pl.pallas_call(
        outputs_kernel,
        out_shape=[jax.ShapeDtypeStruct((rows_dev, cols_dev), BF16)] * 2
        + [jax.ShapeDtypeStruct((frows, rank), F32)],
        in_specs=[whole] * 5,
        out_specs=[hbm] * 3,
        scratch_shapes=[pltpu.VMEM((rows_dev // step, step, cols_dev), BF16)] * 2
        + [sem(2, rows_dev // step), pltpu.SemaphoreType.DMA],
        compiler_params=pltpu.CompilerParams(vmem_limit_bytes=32 * 1024 * 1024),
        name="momentum_and_update",
    )(buffer, basis, scaled, coeff, new_right)


def solution(mesh, nx=X_CHIPS):
    placed = (P("row", "col"), P("row", "col"), P(("col", "row"), None))
    return jax.shard_map(
        functools.partial(body, nx), mesh=mesh, in_specs=placed, out_specs=placed, check_vma=False
    )
```

time: 577 us -> 92.2 us (0.16)
  the two profiles are of different devices: /device:TPU:32 before, /device:TPU:1 now
where the time goes in v1:
time: 92.2 us; the launch traced here: 92.1 us
  Pallas kernels  91.4 us (99%)
    pallas_call x1, Pallas kernels, body(): pl.pallas_call(functools.partial(step_kernel, (ny, nx, nz, scale)), out_s...  89.7 us

profile of v1, /device:TPU:1, one launch (start us, length us, event | category | flops | bytes accessed | tf_op | source)
XLA Modules:
  0.0 92.1 jit_solution(11909439548433728275)
XLA Ops:
  0.6 89.7 %panel_and_factor.1 = (bf16[512,1152]{1,0:T(8,128)(2,1)S(1)}, bf16[512,256]{1,0:T(8,128)(2,1)S(1)}, bf16[512,256]{1,0:T(8,128)(2,1)S(1)}, bf16[256,1152]{1,0:T(8,128)(2,1)S(1)}, f32[72,256]{1,0:T(8,128)S(1)}) custom-call(bf16[512,1152]{1,0:T(8,128)(2,1)} %momentum.1, bf16[512,1152]{1,0:T(8,128)(2,1)} %gradient.1, f32[72,256]{1,0:T(8,128)} %factor.1), custom_call_target="tpu_custom_call" | custom-call | tf_op jit(solution)/shard_map/panel_and_factor/pallas_call | solution.py:448
  90.3 1.8 %momentum_and_update.1 = (bf16[512,1152]{1,0:T(8,128)(2,1)}, bf16[512,1152]{1,0:T(8,128)(2,1)}, f32[72,256]{1,0:T(8,128)}) custom-call(bf16[512,1152]{1,0:T(8,128)(2,1)S(1)} %get-tuple-element.8.buffer, bf16[512,256]{1,0:T(8,128)(2,1)S(1)} %get-tuple-element.9.basis, bf16[512,256]{1,0:T(8,128)(2,1)S(1)} %get-tuple-element.10.scaled, ...), custom_call_target="tpu_custom_call" | custom-call | tf_op jit(solution)/shard_map/momentum_and_update/pallas_call | solution.py:466

commit v2 on v1

--- a/solution.py
+++ b/solution.py
@@ -88,14 +88,13 @@
     return lax.dot_general(a, b, ((dims[:1], dims[1:]), ((), ())), precision=lax.Precision.HIGHEST)
 
 
-def inverse_lower(work, out_ref, hook):
+def inverse_lower(work, out_ref):
     top, rest = slice(0, LANES), slice(LANES, 2 * LANES)
     first = eliminate(work[top, top])
     out_ref[top, top] = first
     out_ref[top, rest] = jnp.zeros((LANES, LANES), F32)
     upper = exact(first, work[top, rest], (1, 0))
     schur = work[rest, rest] - exact(upper, upper, (0, 0))
-    hook()
     second = eliminate(schur)
     out_ref[rest, rest] = second
     out_ref[rest, top] = -exact(second, exact(upper, first, (0, 0)), (1, 0))
@@ -123,12 +122,12 @@
     (
         grad, fown, fslot, fall, part, psend, xgot, zsend, zgot, panel, panel_t,
         gpart, ggot, gall, work, lower_inv, wpart, wsib, wsibgot, wsend, wgot, wall, coeff_t,
-        nown, nxgot, nmid, nzgot,
+        nown, ngot,
         local_sem, f_send, f_recv, fs_send, fs_recv,
         x_send, x_recv, z_send, z_recv, pz_send, pz_recv, px_send, px_recv,
-        gy_send, gy_recv, gz_send, gz_recv, gx_send, gx_recv, gs_send, gs_recv,
+        gy_send, gy_recv, gx_send, gx_recv, gs_send, gs_recv,
         ws_send, ws_recv, wy_send, wy_recv, wa_send, wa_recv, wf_send, wf_recv,
-        nx_send, nx_recv, nz_send, nz_recv,
+        n_send, n_recv,
     ) = scratch
     row, col = lax.axis_index("row"), lax.axis_index("col")
     y, core = row // 2, row % 2
@@ -148,6 +147,12 @@
     def at_z(d):
         return (row, x * nz + lax.rem(z + d, nz))
 
+    def col_of(dx, dz):
+        return lax.rem(x + dx + nx, nx) * nz + lax.rem(z + dz + nz, nz)
+
+    def at_xz(dx, dz):
+        return (row, col_of(dx, dz))
+
     started = []
 
     def send(copy):
@@ -163,7 +168,9 @@
         copy.start()
 
     peers = [at_y(d, flip) for d in range(ny) for flip in range(2) if (d, flip) != (0, 0)]
-    peers += [at_x(d) for d in range(1, nx)] + [at_z(d) for d in range(1, nz)]
+    col_peers = [(dx, dz) for dx in range(nx) for dz in range(nz) if (dx, dz) != (0, 0)]
+    col_peers.sort(key=lambda d: -min(d[0], nx - d[0]) - min(d[1], nz - d[1]))
+    peers += [at_xz(*d) for d in col_peers]
     barrier = pltpu.get_barrier_semaphore()
     for peer in peers:
         pl.semaphore_signal(barrier, inc=1, device_id=peer, device_id_type=MESH)
@@ -205,69 +212,54 @@
     prow = rows_dev // ncol
     right = fall[...].astype(BF16)
     many = rows_dev // nx
-    halves_z = [pl.ds(h * (nz // 2), nz // 2) for h in range(2)]
+    order = sorted(range(1, nz), key=lambda d: -min(d, nz - d)) + [0]
     for dx in list(range(1, nx)) + [0]:
         group = lax.rem(x + dx, nx)
-        value = dot(buf[pl.ds(pl.multiple_of(group * many, many), many), :], right)
+        value = dot(buf[pl.ds(pl.multiple_of(group * many, many), many), :], right).reshape(nz, prow, rank)
         if dx == 0:
-            part[...] = value.reshape(nz, prow, rank)
+            part[...] = value
             continue
-        psend[dx] = value.astype(BF16).reshape(nz, prow, rank)
-        for h in range(2):
-            src, dst = psend.at[dx, halves_z[h]], xgot.at[dx, halves_z[h]]
-            send(remote(src, dst, x_send.at[dx, h], x_recv.at[dx, h], at_x(dx)))
-    for h in range(2):
-        here = halves_z[h]
-        value = part[here]
+        psend[dx] = value.astype(BF16)
+        for dz in order:
+            src = psend.at[dx, lax.rem(z + dz, nz)]
+            send(remote(src, xgot.at[dx, dz], x_send.at[dx, dz], x_recv.at[dx, dz], at_x(dx)))
+    for dz in order:
+        value = part[lax.rem(z + dz, nz)]
         for dx in range(1, nx):
-            got = xgot.at[dx, here]
-            remote(got, got, x_send.at[dx, h], x_recv.at[dx, h], at_x(dx)).wait_recv()
-            value = value + xgot[dx, here].astype(F32)
-        part[here] = value
-        zsend[here] = value.astype(BF16)
-        for i in range(nz // 2):
-            to = h * (nz // 2) + i
-            away = lax.rem(to - z + nz, nz)
-
-            @pl.when(away != 0)
-            def _(to=to, away=away):
-                copy = remote(zsend.at[to], zgot.at[away], z_send.at[away], z_recv.at[away], (row, x * nz + to))
-                copy.start()
-
-    value = part[z]
-    for dz in range(1, nz):
+            remote(xgot.at[dx, dz], xgot.at[dx, dz], x_send.at[dx, dz], x_recv.at[dx, dz], at_x(dx)).wait_recv()
+            value = value + xgot[dx, dz].astype(F32)
+        if dz:
+            zsend[dz] = value.astype(BF16)
+            send(remote(zsend.at[dz], zgot.at[dz], z_send.at[dz], z_recv.at[dz], at_z(dz)))
+    for dz in sorted(range(1, nz), key=lambda d: min(d, nz - d)):
         remote(zgot.at[dz], zgot.at[dz], z_send.at[dz], z_recv.at[dz], at_z(dz)).wait_recv()
         value = value + zgot[dz].astype(F32)
     panel[col] = value.astype(BF16)
-    for dz in sorted(range(1, nz), key=lambda d: -min(d, nz - d)):
+    for dz in order[:-1]:
         send(remote(panel.at[col], panel.at[col], pz_send.at[dz], pz_recv.at[dz], at_z(dz)))
-    for step in range(2):
-        lot = z // (nz // 2) if step == 0 else 1 - z // (nz // 2)
-        for i in range(nz // 2):
-            source = lot * (nz // 2) + i
-            away = lax.rem(z - source + nz, nz)
-            got = panel.at[x * nz + source]
-
-            @pl.when(away != 0)
-            def _(got=got, away=away):
-                remote(got, got, pz_send.at[away], pz_recv.at[away], at_z(1)).wait_recv()
-
-        group = panel.at[pl.ds(x * nz + lot * (nz // 2), nz // 2)]
+    for dz in [0] + sorted(range(1, nz), key=lambda d: min(d, nz - d)):
+        piece = x * nz + lax.rem(z + nz - dz, nz)
+        if dz:
+            remote(panel.at[piece], panel.at[piece], pz_send.at[dz], pz_recv.at[dz], at_z(dz)).wait_recv()
         for dx in range(1, nx):
-            send(remote(group, group, px_send.at[dx, step], px_recv.at[dx, step], at_x(dx)))
-    for step in range(2):
-        lot = z // (nz // 2) if step == 0 else 1 - z // (nz // 2)
+            send(remote(panel.at[piece], panel.at[piece], px_send.at[dx, dz], px_recv.at[dx, dz], at_x(dx)))
+    for dz in range(nz):
         for dx in range(1, nx):
-            group = panel.at[pl.ds(lax.rem(x + nx - dx, nx) * nz + lot * (nz // 2), nz // 2)]
-            remote(group, group, px_send.at[dx, step], px_recv.at[dx, step], at_x(dx)).wait_recv()
-    for dz in range(1, nz):
-        got = zsend.at[lax.rem(z + dz, nz)]
-        remote(got, got, z_send.at[dz], z_recv.at[dz], at_z(dz)).wait_send()
+            piece = lax.rem(x + nx - dx, nx) * nz + lax.rem(z + nz - dz, nz)
+            remote(panel.at[piece], panel.at[piece], px_send.at[dx, dz], px_recv.at[dx, dz], at_x(dx)).wait_recv()
 
     left = panel[...].reshape(rows_dev, rank)
     left_t = left.T
     halves = rank // 2
     panel_t[...] = left_t.reshape(2, halves, rows_dev)
+
+    wrow = halves // ny
+    value = dot(panel_t[1 - core], buf[...])
+    wsib[...] = value.astype(BF16).reshape(ny, wrow, cols_dev)
+    for d in sorted(range(ny), key=lambda d: -min(d, ny - d)):
+        piece = lax.rem(y + d, ny)
+        send(remote(wsib.at[piece], wsibgot.at[d], ws_send.at[d], ws_recv.at[d], sibling))
+
     grow = rank // ncol
     gram = dot(left_t, left)
     for h in range(2):
@@ -277,62 +269,48 @@
         half = core if flip == 0 else 1 - core
         send(remote(gpart.at[half, col], ggot.at[d, flip], gy_send.at[d, flip], gy_recv.at[d, flip], at_y(d, flip)))
 
-    wrow = halves // ny
-    value = dot(panel_t[1 - core], buf[...])
-    wsib[...] = value.astype(BF16).reshape(ny, wrow, cols_dev)
-    for d in list(range(1, ny)) + [0]:
-        piece = lax.rem(y + d, ny)
-        send(remote(wsib.at[piece], wsibgot.at[d], ws_send.at[d], ws_recv.at[d], sibling))
     value = dot(panel_t[core], buf[...])
     wpart[...] = value.reshape(ny, wrow, cols_dev)
+
+    def merged(d):
+        remote(wsibgot.at[d], wsibgot.at[d], ws_send.at[d], ws_recv.at[d], sibling).wait_recv()
+        return wpart[lax.rem(y + d, ny)] + wsibgot[d].astype(F32)
+
+    for d in sorted(range(1, ny), key=lambda d: -min(d, ny - d)):
+        wsend[d] = merged(d).astype(BF16)
+        send(remote(wsend.at[d], wgot.at[d], wy_send.at[d], wy_recv.at[d], at_y(d)))
 
     value = gpart[core, col]
     for d, flip in gpeers:
         remote(ggot.at[d, flip], ggot.at[d, flip], gy_send.at[d, flip], gy_recv.at[d, flip], at_y(d, flip)).wait_recv()
         value = value + ggot[d, flip]
     gall[core, col] = value
-    for dz in range(1, nz):
-        send(remote(gall.at[core, col], gall.at[core, col], gz_send.at[dz], gz_recv.at[dz], at_z(dz)))
-
-    def merged(d):
-        remote(wsibgot.at[d], wsibgot.at[d], ws_send.at[d], ws_recv.at[d], sibling).wait_recv()
-        return wpart[lax.rem(y + d, ny)] + wsibgot[d].astype(F32)
-
+    slice_own = gall.at[core, col]
+    for dx, dz in col_peers:
+        send(remote(slice_own, slice_own, gx_send.at[dx, dz], gx_recv.at[dx, dz], at_xz(dx, dz)))
+    for dx, dz in col_peers[::-1]:
+        piece = gall.at[core, col_of(-dx, -dz)]
+        remote(piece, piece, gx_send.at[dx, dz], gx_recv.at[dx, dz], at_xz(dx, dz)).wait_recv()
+    send(remote(gall.at[core], gall.at[core], gs_send.at[0], gs_recv.at[0], sibling))
+    value = merged(0)
+    for d in range(1, ny):
+        remote(wgot.at[d], wgot.at[d], wy_send.at[d], wy_recv.at[d], at_y(d)).wait_recv()
+        value = value + wgot[d].astype(F32)
+    mine = core * ny + y
+    wall[mine] = value.astype(BF16)
     for d in sorted(range(1, ny), key=lambda d: -min(d, ny - d)):
-        wsend[d] = merged(d).astype(BF16)
-        send(remote(wsend.at[d], wgot.at[d], wy_send.at[d], wy_recv.at[d], at_y(d)))
-
-    for dz in range(1, nz):
-        got = gall.at[core, x * nz + lax.rem(z + nz - dz, nz)]
-        remote(got, got, gz_send.at[dz], gz_recv.at[dz], at_z(dz)).wait_recv()
-    group = gall.at[core, pl.ds(x * nz, nz)]
-    for dx in range(1, nx):
-        send(remote(group, group, gx_send.at[dx], gx_recv.at[dx], at_x(dx)))
-    for dx in range(1, nx):
-        group = gall.at[core, pl.ds(lax.rem(x + nx - dx, nx) * nz, nz)]
-        remote(group, group, gx_send.at[dx], gx_recv.at[dx], at_x(dx)).wait_recv()
-    send(remote(gall.at[core], gall.at[core], gs_send.at[0], gs_recv.at[0], sibling))
+        send(remote(wall.at[mine], wall.at[mine], wa_send.at[d], wa_recv.at[d], at_y(d)))
+    send(remote(wall.at[mine], wall.at[mine], wf_send.at[0], wf_recv.at[0], sibling))
     remote(gall.at[1 - core], gall.at[1 - core], gs_send.at[0], gs_recv.at[0], sibling).wait_recv()
     for h in range(2):
         work[:, h * LANES : (h + 1) * LANES] = gall[h].reshape(rank, LANES)
-    def finish_sum():
-        value = merged(0)
-        for d in range(1, ny):
-            remote(wgot.at[d], wgot.at[d], wy_send.at[d], wy_recv.at[d], at_y(d)).wait_recv()
-            value = value + wgot[d].astype(F32)
-        mine = core * ny + y
-        wall[mine] = value.astype(BF16)
-        for d in sorted(range(1, ny), key=lambda d: -min(d, ny - d)):
-            send(remote(wall.at[mine], wall.at[mine], wa_send.at[d], wa_recv.at[d], at_y(d)))
-        send(remote(wall.at[mine], wall.at[mine], wf_send.at[0], wf_recv.at[0], sibling))
-
     def forward():
         for d in near:
             piece = core * ny + lax.rem(y + ny - d, ny)
             remote(wall.at[piece], wall.at[piece], wa_send.at[d], wa_recv.at[d], at_y(d)).wait_recv()
             send(remote(wall.at[piece], wall.at[piece], wf_send.at[d], wf_recv.at[d], sibling))
 
-    inverse_lower(work, lower_inv, finish_sum)
+    inverse_lower(work, lower_inv)
     forward()
     high, low = split(lower_inv[...])
     basis = dot_nt(left, high) + dot_nt(left, low)
@@ -347,32 +325,26 @@
     for i in range(cols_dev // LANES):
         value = coeff_t[:, i * LANES : (i + 1) * LANES]
         squares = squares + value * value
-    sums = squares.T
-    value = sums[0:8]
-    for i in range(1, LANES // 8):
-        value = value + sums[8 * i : 8 * i + 8]
+    value = jnp.sum(squares.T, axis=0, keepdims=True)
     nown[...] = value
-    for dx in range(1, nx):
-        send(remote(nown, nxgot.at[dx], nx_send.at[dx], nx_recv.at[dx], at_x(dx)))
+    for dx, dz in col_peers:
+        send(remote(nown, ngot.at[dx, dz], n_send.at[dx, dz], n_recv.at[dx, dz], at_xz(dx, dz)))
     coeff_low[...] = coeff_t[...].astype(BF16)
-    for dx in range(1, nx):
-        remote(nxgot.at[dx], nxgot.at[dx], nx_send.at[dx], nx_recv.at[dx], at_x(dx)).wait_recv()
-        value = value + nxgot[dx]
-    nmid[...] = value
-    for dz in range(1, nz):
-        send(remote(nmid, nzgot.at[dz], nz_send.at[dz], nz_recv.at[dz], at_z(dz)))
-    pick = lax.broadcasted_iota(jnp.int32, (frows, cols_dev), 1)
-    pick = pick == lax.broadcasted_iota(jnp.int32, (frows, cols_dev), 0) + row * frows
-    pick = jnp.where(pick, 1.0, 0.0).astype(BF16)
-    c_high, c_low = split(coeff_t[...])
-    mine = dot_nt(pick, c_high) + dot_nt(pick, c_low)
+    begin = row * frows
+    if cols_dev >= 2 * LANES:
+        tile = jnp.minimum(begin // LANES, cols_dev // LANES - 2)
+        near = coeff_t[:, pl.ds(pl.multiple_of(tile * LANES, LANES), 2 * LANES)]
+        near = pltpu.roll(near, 2 * LANES - (begin - tile * LANES), axis=1)
+    else:
+        near = pltpu.roll(coeff_t[...], cols_dev - begin, axis=1)
+    mine = near[:, :LANES].T[:frows]
     for copy in started:
         copy.wait_send()
-    for dz in range(1, nz):
-        remote(nzgot.at[dz], nzgot.at[dz], nz_send.at[dz], nz_recv.at[dz], at_z(dz)).wait_recv()
-        value = value + nzgot[dz]
-    norms = jnp.sum(value, axis=0, keepdims=True)
-    inverse = 1.0 / jnp.sqrt(norms + 1e-06)
+    for dx, dz in col_peers[::-1]:
+        got = ngot.at[dx, dz]
+        remote(got, got, n_send.at[dx, dz], n_recv.at[dx, dz], at_xz(dx, dz)).wait_recv()
+        value = value + ngot[dx, dz]
+    inverse = 1.0 / jnp.sqrt(value + 1e-06)
     right_out[...] = mine * inverse
     scaled_out[...] = (basis * (inverse * scale)).astype(BF16)
 
@@ -429,16 +401,14 @@
         pltpu.VMEM((ny, wrow, cols_dev), BF16),
         pltpu.VMEM((2 * ny, wrow, cols_dev), BF16),
         pltpu.VMEM((rank, cols_dev), F32),
-        pltpu.VMEM((8, rank), F32),
-        pltpu.VMEM((nx, 8, rank), F32),
-        pltpu.VMEM((8, rank), F32),
-        pltpu.VMEM((nz, 8, rank), F32),
+        pltpu.VMEM((1, rank), F32),
+        pltpu.VMEM((nx, nz, 1, rank), F32),
         sem(3),
         sem(ny), sem(ny), sem(ny), sem(ny),
-        sem(nx, 2), sem(nx, 2), sem(nz), sem(nz), sem(nz), sem(nz), sem(nx, 2), sem(nx, 2),
-        sem(ny, 2), sem(ny, 2), sem(nz), sem(nz), sem(nx), sem(nx), sem(1), sem(1),
+        sem(nx, nz), sem(nx, nz), sem(nz), sem(nz), sem(nz), sem(nz), sem(nx, nz), sem(nx, nz),
+        sem(ny, 2), sem(ny, 2), sem(nx, nz), sem(nx, nz), sem(1), sem(1),
         sem(ny), sem(ny), sem(ny), sem(ny), sem(ny), sem(ny), sem(ny), sem(ny),
-        sem(nx), sem(nx), sem(nz), sem(nz),
+        sem(nx, nz), sem(nx, nz),
     ]
     momentum, gradient, right_factor = [
         pltpu.with_memory_space_constraint(value, pltpu.HBM) for value in (momentum, gradient, right_factor)

time: 92.2 us -> 82.3 us (0.89)
  Pallas kernels: 91.4 us -> 81.5 us
    pallas_call x1, Pallas kernels: 89.7 us -> 79.8 us  [body(): pl.pallas_call(functools.partial(step_kernel, (ny, nx, nz, scale)), out_s...]
where the time goes in v2:
time: 82.3 us; the launch traced here: 82.2 us
  Pallas kernels  81.5 us (99%)
    pallas_call x1, Pallas kernels, body(): pl.pallas_call(functools.partial(step_kernel, (ny, nx, nz, scale)), out_s...  79.8 us
    pallas_call x1, Pallas kernels, body(): pl.pallas_call(outputs_kernel, out_shape=[jax.ShapeDtypeStruct((rows_dev,...  1.76 us

profile of v2, /device:TPU:1, one launch (start us, length us, event | category | flops | bytes accessed | tf_op | source)
XLA Modules:
  0.0 82.2 jit_solution(2999069046310937129)
XLA Ops:
  0.6 79.8 %panel_and_factor.1 = (bf16[512,1152]{1,0:T(8,128)(2,1)S(1)}, bf16[512,256]{1,0:T(8,128)(2,1)S(1)}, bf16[512,256]{1,0:T(8,128)(2,1)S(1)}, bf16[256,1152]{1,0:T(8,128)(2,1)S(1)}, f32[72,256]{1,0:T(8,128)S(1)}) custom-call(bf16[512,1152]{1,0:T(8,128)(2,1)} %momentum.1, bf16[512,1152]{1,0:T(8,128)(2,1)} %gradient.1, f32[72,256]{1,0:T(8,128)} %factor.1), custom_call_target="tpu_custom_call" | custom-call | tf_op jit(solution)/shard_map/panel_and_factor/pallas_call | solution.py:418
  80.4 1.8 %momentum_and_update.1 = (bf16[512,1152]{1,0:T(8,128)(2,1)}, bf16[512,1152]{1,0:T(8,128)(2,1)}, f32[72,256]{1,0:T(8,128)}) custom-call(bf16[512,1152]{1,0:T(8,128)(2,1)S(1)} %get-tuple-element.8.buffer, bf16[512,256]{1,0:T(8,128)(2,1)S(1)} %get-tuple-element.9.basis, bf16[512,256]{1,0:T(8,128)(2,1)S(1)} %get-tuple-element.10.scaled, ...), custom_call_target="tpu_custom_call" | custom-call | tf_op jit(solution)/shard_map/momentum_and_update/pallas_call | solution.py:436

commit v3 on v2

--- a/solution.py
+++ b/solution.py
@@ -88,13 +88,14 @@
     return lax.dot_general(a, b, ((dims[:1], dims[1:]), ((), ())), precision=lax.Precision.HIGHEST)
 
 
-def inverse_lower(work, out_ref):
+def inverse_lower(work, out_ref, hook):
     top, rest = slice(0, LANES), slice(LANES, 2 * LANES)
     first = eliminate(work[top, top])
     out_ref[top, top] = first
     out_ref[top, rest] = jnp.zeros((LANES, LANES), F32)
     upper = exact(first, work[top, rest], (1, 0))
     schur = work[rest, rest] - exact(upper, upper, (0, 0))
+    hook()
     second = eliminate(schur)
     out_ref[rest, rest] = second
     out_ref[rest, top] = -exact(second, exact(upper, first, (0, 0)), (1, 0))
@@ -121,13 +122,13 @@
     ny, nx, nz, scale = sizes
     (
         grad, fown, fslot, fall, part, psend, xgot, zsend, zgot, panel, panel_t,
-        gpart, ggot, gall, work, lower_inv, wpart, wsib, wsibgot, wsend, wgot, wall, coeff_t,
+        gpart, ggot, gall, work, lower_inv, wpart, wsib, wsibgot, wsend, wgot, wrelay, wall, coeff_t,
         nown, ngot,
         local_sem, f_send, f_recv, fs_send, fs_recv,
         x_send, x_recv, z_send, z_recv, pz_send, pz_recv, px_send, px_recv,
         gy_send, gy_recv, gx_send, gx_recv, gs_send, gs_recv,
         ws_send, ws_recv, wy_send, wy_recv, wa_send, wa_recv, wf_send, wf_recv,
-        n_send, n_recv,
+        n_send, n_recv, wr_send, wr_recv, relay_send,
     ) = scratch
     row, col = lax.axis_index("row"), lax.axis_index("col")
     y, core = row // 2, row % 2
@@ -153,11 +154,29 @@
     def at_xz(dx, dz):
         return (row, col_of(dx, dz))
 
-    started = []
+    started, some_started = [], []
 
     def send(copy):
         copy.start()
         started.append(copy)
+
+    def send_if(condition, copy):
+        pl.when(condition)(lambda: copy.start())
+        some_started.append((condition, copy))
+
+    half_way = ny // 2
+    relays = ny >= 4
+    far_first = sorted(range(1, ny), key=lambda d: -min(d, ny - d))
+    near = sorted(range(1, ny), key=lambda d: min(d, ny - d))
+    if relays:
+        far_first = [ny - 1] + [d for d in far_first if d != ny - 1]
+        near = [ny - 1] + [d for d in near if d != ny - 1]
+
+    def send_y(d, copy):
+        if d == half_way and relays:
+            send_if(core == 0, copy)
+        else:
+            send(copy)
 
     loads = [
         pltpu.make_async_copy(momentum, buf, local_sem.at[0]),
@@ -178,8 +197,8 @@
     fslot[row] = jnp.concatenate([fown[:, :LANES], fown[:, LANES:]], axis=0).astype(BF16)
     pl.semaphore_wait(barrier, len(peers))
 
-    for d in sorted(range(1, ny), key=lambda d: -min(d, ny - d)):
-        send(remote(fslot.at[row], fslot.at[row], f_send.at[d], f_recv.at[d], at_y(d)))
+    for d in far_first:
+        send_y(d, remote(fslot.at[row], fslot.at[row], f_send.at[d], f_recv.at[d], at_y(d)))
     send(remote(fslot.at[row], fslot.at[row], fs_send.at[0], fs_recv.at[0], sibling))
     loads[0].wait()
     loads[1].wait()
@@ -198,10 +217,13 @@
         fall[here, LANES:] = whole[frows:]
 
     unpack(row)
-    near = sorted(range(1, ny), key=lambda d: min(d, ny - d))
     for d in near:
         source = lax.rem(y + ny - d, ny) * 2 + core
         remote(fslot.at[source], fslot.at[source], f_send.at[d], f_recv.at[d], at_y(ny - d)).wait_recv()
+        if d == ny - 1 and relays:
+            block = fslot.at[source]
+            copy = remote(block, block, relay_send.at[0], f_recv.at[half_way], at_y(half_way + 1))
+            send_if(core == 1, copy)
         send(remote(fslot.at[source], fslot.at[source], fs_send.at[d], fs_recv.at[d], sibling))
         unpack(source)
     for d in [0] + near:
@@ -254,11 +276,14 @@
     panel_t[...] = left_t.reshape(2, halves, rows_dev)
 
     wrow = halves // ny
-    value = dot(panel_t[1 - core], buf[...])
-    wsib[...] = value.astype(BF16).reshape(ny, wrow, cols_dev)
-    for d in sorted(range(ny), key=lambda d: -min(d, ny - d)):
-        piece = lax.rem(y + d, ny)
-        send(remote(wsib.at[piece], wsibgot.at[d], ws_send.at[d], ws_recv.at[d], sibling))
+    tiles = cols_dev // LANES
+    cuts = [0, (tiles + 1) // 2 * LANES, cols_dev] if tiles > 1 else [0, cols_dev]
+    parts = [pl.ds(a, b - a) for a, b in zip(cuts[:-1], cuts[1:])]
+    for p, lot in enumerate(parts):
+        value = dot(panel_t[1 - core], buf[:, lot])
+        wsib[:, :, lot] = value.astype(BF16).reshape(ny, wrow, lot.size)
+        src, dst = wsib.at[:, :, lot], wsibgot.at[:, :, lot]
+        send(remote(src, dst, ws_send.at[p], ws_recv.at[p], sibling))
 
     grow = rank // ncol
     gram = dot(left_t, left)
@@ -272,14 +297,45 @@
     value = dot(panel_t[core], buf[...])
     wpart[...] = value.reshape(ny, wrow, cols_dev)
 
-    def merged(d):
-        remote(wsibgot.at[d], wsibgot.at[d], ws_send.at[d], ws_recv.at[d], sibling).wait_recv()
-        return wpart[lax.rem(y + d, ny)] + wsibgot[d].astype(F32)
-
-    for d in sorted(range(1, ny), key=lambda d: -min(d, ny - d)):
-        wsend[d] = merged(d).astype(BF16)
-        send(remote(wsend.at[d], wgot.at[d], wy_send.at[d], wy_recv.at[d], at_y(d)))
-
+    def merged(d, lot):
+        piece = lax.rem(y + d, ny)
+        return wpart[piece, :, lot] + wsibgot[piece, :, lot].astype(F32)
+
+    for p, lot in enumerate(parts):
+        got = wsibgot.at[:, :, lot]
+        remote(got, got, ws_send.at[p], ws_recv.at[p], sibling).wait_recv()
+        for d in far_first:
+            wsend[d, :, lot] = merged(d, lot).astype(BF16)
+            src = wsend.at[d, :, lot]
+            send_y(d, remote(src, wgot.at[d, :, lot], wy_send.at[d, p], wy_recv.at[d, p], at_y(d)))
+            if d == half_way and relays:
+                copy = remote(src, wrelay.at[:, lot], wr_send.at[p], wr_recv.at[p], at_y(ny - 1))
+                send_if(core == 1, copy)
+
+    def pass_on(p, lot):
+        if not relays:
+            return
+        got = wrelay.at[:, lot]
+        arriving = remote(got, got, wr_send.at[p], wr_recv.at[p], at_y(ny - 1))
+        pl.when(core == 1)(lambda: arriving.wait_recv())
+        copy = remote(got, wgot.at[half_way, :, lot], relay_send.at[1 + p], wy_recv.at[half_way, p], at_y(half_way + 1))
+        send_if(core == 1, copy)
+
+    mine = core * ny + y
+
+    def finish(p, lot):
+        value = merged(0, lot)
+        for d in near:
+            got = wgot.at[d, :, lot]
+            remote(got, got, wy_send.at[d, p], wy_recv.at[d, p], at_y(d)).wait_recv()
+            value = value + wgot[d, :, lot].astype(F32)
+        wall[mine, :, lot] = value.astype(BF16)
+        block = wall.at[mine, :, lot]
+        for d in far_first:
+            send_y(d, remote(block, block, wa_send.at[d, p], wa_recv.at[d, p], at_y(d)))
+
+    for p, lot in enumerate(parts):
+        pass_on(p, lot)
     value = gpart[core, col]
     for d, flip in gpeers:
         remote(ggot.at[d, flip], ggot.at[d, flip], gy_send.at[d, flip], gy_recv.at[d, flip], at_y(d, flip)).wait_recv()
@@ -288,29 +344,37 @@
     slice_own = gall.at[core, col]
     for dx, dz in col_peers:
         send(remote(slice_own, slice_own, gx_send.at[dx, dz], gx_recv.at[dx, dz], at_xz(dx, dz)))
+    for p, lot in enumerate(parts[:-1]):
+        finish(p, lot)
     for dx, dz in col_peers[::-1]:
         piece = gall.at[core, col_of(-dx, -dz)]
         remote(piece, piece, gx_send.at[dx, dz], gx_recv.at[dx, dz], at_xz(dx, dz)).wait_recv()
     send(remote(gall.at[core], gall.at[core], gs_send.at[0], gs_recv.at[0], sibling))
-    value = merged(0)
-    for d in range(1, ny):
-        remote(wgot.at[d], wgot.at[d], wy_send.at[d], wy_recv.at[d], at_y(d)).wait_recv()
-        value = value + wgot[d].astype(F32)
-    mine = core * ny + y
-    wall[mine] = value.astype(BF16)
-    for d in sorted(range(1, ny), key=lambda d: -min(d, ny - d)):
-        send(remote(wall.at[mine], wall.at[mine], wa_send.at[d], wa_recv.at[d], at_y(d)))
+    finish(len(parts) - 1, parts[-1])
     send(remote(wall.at[mine], wall.at[mine], wf_send.at[0], wf_recv.at[0], sibling))
     remote(gall.at[1 - core], gall.at[1 - core], gs_send.at[0], gs_recv.at[0], sibling).wait_recv()
     for h in range(2):
         work[:, h * LANES : (h + 1) * LANES] = gall[h].reshape(rank, LANES)
+
+    def arrive(d):
+        piece = core * ny + lax.rem(y + ny - d, ny)
+        for p, lot in enumerate(parts):
+            block = wall.at[piece, :, lot]
+            remote(block, block, wa_send.at[d, p], wa_recv.at[d, p], at_y(d)).wait_recv()
+            if d == ny - 1 and relays:
+                copy = remote(block, block, relay_send.at[3 + p], wa_recv.at[half_way, p], at_y(half_way + 1))
+                send_if(core == 1, copy)
+        send(remote(wall.at[piece], wall.at[piece], wf_send.at[d], wf_recv.at[d], sibling))
+
     def forward():
-        for d in near:
-            piece = core * ny + lax.rem(y + ny - d, ny)
-            remote(wall.at[piece], wall.at[piece], wa_send.at[d], wa_recv.at[d], at_y(d)).wait_recv()
-            send(remote(wall.at[piece], wall.at[piece], wf_send.at[d], wf_recv.at[d], sibling))
-
-    inverse_lower(work, lower_inv)
+        for d in near[1:] if relays else near:
+            arrive(d)
+
+    def hook():
+        if relays:
+            arrive(near[0])
+
+    inverse_lower(work, lower_inv, hook)
     forward()
     high, low = split(lower_inv[...])
     basis = dot_nt(left, high) + dot_nt(left, low)
@@ -340,6 +404,8 @@
     mine = near[:, :LANES].T[:frows]
     for copy in started:
         copy.wait_send()
+    for condition, copy in some_started:
+        pl.when(condition)(lambda copy=copy: copy.wait_send())
     for dx, dz in col_peers[::-1]:
         got = ngot.at[dx, dz]
         remote(got, got, n_send.at[dx, dz], n_recv.at[dx, dz], at_xz(dx, dz)).wait_recv()
@@ -399,6 +465,7 @@
         pltpu.VMEM((ny, wrow, cols_dev), BF16),
         pltpu.VMEM((ny, wrow, cols_dev), BF16),
         pltpu.VMEM((ny, wrow, cols_dev), BF16),
+        pltpu.VMEM((wrow, cols_dev), BF16),
         pltpu.VMEM((2 * ny, wrow, cols_dev), BF16),
         pltpu.VMEM((rank, cols_dev), F32),
         pltpu.VMEM((1, rank), F32),
@@ -407,8 +474,8 @@
         sem(ny), sem(ny), sem(ny), sem(ny),
         sem(nx, nz), sem(nx, nz), sem(nz), sem(nz), sem(nz), sem(nz), sem(nx, nz), sem(nx, nz),
         sem(ny, 2), sem(ny, 2), sem(nx, nz), sem(nx, nz), sem(1), sem(1),
-        sem(ny), sem(ny), sem(ny), sem(ny), sem(ny), sem(ny), sem(ny), sem(ny),
-        sem(nx, nz), sem(nx, nz),
+        sem(2), sem(2), sem(ny, 2), sem(ny, 2), sem(ny, 2), sem(ny, 2), sem(ny), sem(ny),
+        sem(nx, nz), sem(nx, nz), sem(2), sem(2), sem(5),
     ]
     momentum, gradient, right_factor = [
         pltpu.with_memory_space_constraint(value, pltpu.HBM) for value in (momentum, gradient, right_factor)

time: 82.3 us -> 83.3 us (1.012)
  Pallas kernels: 81.5 us -> 82.5 us
    pallas_call x1, Pallas kernels: 79.8 us -> 80.7 us  [body(): pl.pallas_call(functools.partial(step_kernel, (ny, nx, nz, scale)), out_s...]
where the time goes in v3:
time: 83.3 us; the launch traced here: 83.1 us
  Pallas kernels  82.5 us (99%)
    pallas_call x1, Pallas kernels, body(): pl.pallas_call(functools.partial(step_kernel, (ny, nx, nz, scale)), out_s...  80.7 us
    pallas_call x1, Pallas kernels, body(): pl.pallas_call(outputs_kernel, out_shape=[jax.ShapeDtypeStruct((rows_dev,...  1.75 us

profile of v3, /device:TPU:1, one launch (start us, length us, event | category | flops | bytes accessed | tf_op | source)
XLA Modules:
  0.0 83.1 jit_solution(5170623394645095794)
XLA Ops:
  0.6 80.7 %panel_and_factor.1 = (bf16[512,1152]{1,0:T(8,128)(2,1)S(1)}, bf16[512,256]{1,0:T(8,128)(2,1)S(1)}, bf16[512,256]{1,0:T(8,128)(2,1)S(1)}, bf16[256,1152]{1,0:T(8,128)(2,1)S(1)}, f32[72,256]{1,0:T(8,128)S(1)}) custom-call(bf16[512,1152]{1,0:T(8,128)(2,1)} %momentum.1, bf16[512,1152]{1,0:T(8,128)(2,1)} %gradient.1, f32[72,256]{1,0:T(8,128)} %factor.1), custom_call_target="tpu_custom_call" | custom-call | tf_op jit(solution)/shard_map/panel_and_factor/pallas_call | solution.py:485
  81.4 1.8 %momentum_and_update.1 = (bf16[512,1152]{1,0:T(8,128)(2,1)}, bf16[512,1152]{1,0:T(8,128)(2,1)}, f32[72,256]{1,0:T(8,128)}) custom-call(bf16[512,1152]{1,0:T(8,128)(2,1)S(1)} %get-tuple-element.8.buffer, bf16[512,256]{1,0:T(8,128)(2,1)S(1)} %get-tuple-element.9.basis, bf16[512,256]{1,0:T(8,128)(2,1)S(1)} %get-tuple-element.10.scaled, ...), custom_call_target="tpu_custom_call" | custom-call | tf_op jit(solution)/shard_map/momentum_and_update/pallas_call | solution.py:503

commit v4 on v2

--- a/solution.py
+++ b/solution.py
@@ -32,12 +32,14 @@
     return jnp.broadcast_to(rows[:, lane : lane + 1], (rows.shape[0], LANES))
 
 
-def eliminate(block):
+def eliminate(block, hook=None):
     n = LANES
     lanes = lax.broadcasted_iota(jnp.int32, (8, LANES), 1)
     sublane = lax.broadcasted_iota(jnp.int32, (8, LANES), 0)
     groups = [block[8 * g : 8 * g + 8, :] for g in range(n // 8)]
     for j in range(n // 8):
+        if hook is not None and j == n // 16:
+            hook()
         base = 8 * j
         inside = (lanes >= base) & (lanes < base + 8)
         rows = [jnp.broadcast_to(groups[j][k : k + 1, :], (8, LANES)) for k in range(8)]
@@ -85,17 +87,22 @@
 
 
 def exact(a, b, dims):
-    return lax.dot_general(a, b, ((dims[:1], dims[1:]), ((), ())), precision=lax.Precision.HIGHEST)
-
-
-def inverse_lower(work, out_ref):
+    a_high, a_low = split(a)
+    b_high, b_low = split(b)
+    product = functools.partial(
+        lax.dot_general, dimension_numbers=((dims[:1], dims[1:]), ((), ())), preferred_element_type=F32
+    )
+    return product(a_high, b_high) + (product(a_high, b_low) + product(a_low, b_high))
+
+
+def inverse_lower(work, out_ref, hook):
     top, rest = slice(0, LANES), slice(LANES, 2 * LANES)
     first = eliminate(work[top, top])
     out_ref[top, top] = first
     out_ref[top, rest] = jnp.zeros((LANES, LANES), F32)
     upper = exact(first, work[top, rest], (1, 0))
     schur = work[rest, rest] - exact(upper, upper, (0, 0))
-    second = eliminate(schur)
+    second = eliminate(schur, hook)
     out_ref[rest, rest] = second
     out_ref[rest, top] = -exact(second, exact(upper, first, (0, 0)), (1, 0))
 
@@ -159,6 +166,9 @@
         copy.start()
         started.append(copy)
 
+    far_first = sorted(range(1, ny), key=lambda d: -min(d, ny - d))
+    near = far_first[::-1]
+
     loads = [
         pltpu.make_async_copy(momentum, buf, local_sem.at[0]),
         pltpu.make_async_copy(gradient, grad, local_sem.at[1]),
@@ -178,7 +188,7 @@
     fslot[row] = jnp.concatenate([fown[:, :LANES], fown[:, LANES:]], axis=0).astype(BF16)
     pl.semaphore_wait(barrier, len(peers))
 
-    for d in sorted(range(1, ny), key=lambda d: -min(d, ny - d)):
+    for d in far_first:
         send(remote(fslot.at[row], fslot.at[row], f_send.at[d], f_recv.at[d], at_y(d)))
     send(remote(fslot.at[row], fslot.at[row], fs_send.at[0], fs_recv.at[0], sibling))
     loads[0].wait()
@@ -198,7 +208,6 @@
         fall[here, LANES:] = whole[frows:]
 
     unpack(row)
-    near = sorted(range(1, ny), key=lambda d: min(d, ny - d))
     for d in near:
         source = lax.rem(y + ny - d, ny) * 2 + core
         remote(fslot.at[source], fslot.at[source], f_send.at[d], f_recv.at[d], at_y(ny - d)).wait_recv()
@@ -253,13 +262,6 @@
     halves = rank // 2
     panel_t[...] = left_t.reshape(2, halves, rows_dev)
 
-    wrow = halves // ny
-    value = dot(panel_t[1 - core], buf[...])
-    wsib[...] = value.astype(BF16).reshape(ny, wrow, cols_dev)
-    for d in sorted(range(ny), key=lambda d: -min(d, ny - d)):
-        piece = lax.rem(y + d, ny)
-        send(remote(wsib.at[piece], wsibgot.at[d], ws_send.at[d], ws_recv.at[d], sibling))
-
     grow = rank // ncol
     gram = dot(left_t, left)
     for h in range(2):
@@ -269,17 +271,45 @@
         half = core if flip == 0 else 1 - core
         send(remote(gpart.at[half, col], ggot.at[d, flip], gy_send.at[d, flip], gy_recv.at[d, flip], at_y(d, flip)))
 
+    wrow = halves // ny
+    tiles = cols_dev // LANES
+    cuts = [0, (tiles + 1) // 2 * LANES, cols_dev] if tiles > 1 else [0, cols_dev]
+    parts = [pl.ds(a, b - a) for a, b in zip(cuts[:-1], cuts[1:])]
+    for p, lot in enumerate(parts):
+        value = dot(panel_t[1 - core], buf[:, lot])
+        wsib[:, :, lot] = value.astype(BF16).reshape(ny, wrow, lot.size)
+        src, dst = wsib.at[:, :, lot], wsibgot.at[:, :, lot]
+        send(remote(src, dst, ws_send.at[p], ws_recv.at[p], sibling))
+
     value = dot(panel_t[core], buf[...])
     wpart[...] = value.reshape(ny, wrow, cols_dev)
 
-    def merged(d):
-        remote(wsibgot.at[d], wsibgot.at[d], ws_send.at[d], ws_recv.at[d], sibling).wait_recv()
-        return wpart[lax.rem(y + d, ny)] + wsibgot[d].astype(F32)
-
-    for d in sorted(range(1, ny), key=lambda d: -min(d, ny - d)):
-        wsend[d] = merged(d).astype(BF16)
-        send(remote(wsend.at[d], wgot.at[d], wy_send.at[d], wy_recv.at[d], at_y(d)))
-
+    def merged(d, lot):
+        piece = lax.rem(y + d, ny)
+        return wpart[piece, :, lot] + wsibgot[piece, :, lot].astype(F32)
+
+    def spread(p, lot):
+        got = wsibgot.at[:, :, lot]
+        remote(got, got, ws_send.at[p], ws_recv.at[p], sibling).wait_recv()
+        for d in far_first:
+            wsend[d, :, lot] = merged(d, lot).astype(BF16)
+            src = wsend.at[d, :, lot]
+            send(remote(src, wgot.at[d, :, lot], wy_send.at[d, p], wy_recv.at[d, p], at_y(d)))
+
+    mine = core * ny + y
+
+    def finish(p, lot):
+        value = merged(0, lot)
+        for d in near:
+            got = wgot.at[d, :, lot]
+            remote(got, got, wy_send.at[d, p], wy_recv.at[d, p], at_y(d)).wait_recv()
+            value = value + wgot[d, :, lot].astype(F32)
+        wall[mine, :, lot] = value.astype(BF16)
+        block = wall.at[mine, :, lot]
+        for d in far_first:
+            send(remote(block, block, wa_send.at[d, p], wa_recv.at[d, p], at_y(d)))
+
+    spread(0, parts[0])
     value = gpart[core, col]
     for d, flip in gpeers:
         remote(ggot.at[d, flip], ggot.at[d, flip], gy_send.at[d, flip], gy_recv.at[d, flip], at_y(d, flip)).wait_recv()
@@ -288,33 +318,33 @@
     slice_own = gall.at[core, col]
     for dx, dz in col_peers:
         send(remote(slice_own, slice_own, gx_send.at[dx, dz], gx_recv.at[dx, dz], at_xz(dx, dz)))
+    for p, lot in enumerate(parts[1:]):
+        spread(p + 1, lot)
+    for p, lot in enumerate(parts[:-1]):
+        finish(p, lot)
     for dx, dz in col_peers[::-1]:
         piece = gall.at[core, col_of(-dx, -dz)]
         remote(piece, piece, gx_send.at[dx, dz], gx_recv.at[dx, dz], at_xz(dx, dz)).wait_recv()
     send(remote(gall.at[core], gall.at[core], gs_send.at[0], gs_recv.at[0], sibling))
-    value = merged(0)
-    for d in range(1, ny):
-        remote(wgot.at[d], wgot.at[d], wy_send.at[d], wy_recv.at[d], at_y(d)).wait_recv()
-        value = value + wgot[d].astype(F32)
-    mine = core * ny + y
-    wall[mine] = value.astype(BF16)
-    for d in sorted(range(1, ny), key=lambda d: -min(d, ny - d)):
-        send(remote(wall.at[mine], wall.at[mine], wa_send.at[d], wa_recv.at[d], at_y(d)))
+    finish(len(parts) - 1, parts[-1])
     send(remote(wall.at[mine], wall.at[mine], wf_send.at[0], wf_recv.at[0], sibling))
     remote(gall.at[1 - core], gall.at[1 - core], gs_send.at[0], gs_recv.at[0], sibling).wait_recv()
     for h in range(2):
         work[:, h * LANES : (h + 1) * LANES] = gall[h].reshape(rank, LANES)
+
+    def arrive(d):
+        piece = core * ny + lax.rem(y + ny - d, ny)
+        for p, lot in enumerate(parts):
+            block = wall.at[piece, :, lot]
+            remote(block, block, wa_send.at[d, p], wa_recv.at[d, p], at_y(d)).wait_recv()
+        send(remote(wall.at[piece], wall.at[piece], wf_send.at[d], wf_recv.at[d], sibling))
+
     def forward():
         for d in near:
-            piece = core * ny + lax.rem(y + ny - d, ny)
-            remote(wall.at[piece], wall.at[piece], wa_send.at[d], wa_recv.at[d], at_y(d)).wait_recv()
-            send(remote(wall.at[piece], wall.at[piece], wf_send.at[d], wf_recv.at[d], sibling))
-
-    inverse_lower(work, lower_inv)
-    forward()
+            arrive(d)
+
+    inverse_lower(work, lower_inv, forward)
     high, low = split(lower_inv[...])
-    basis = dot_nt(left, high) + dot_nt(left, low)
-    basis_low[...] = basis.astype(BF16)
     for d in range(ny):
         piece = (1 - core) * ny + lax.rem(y + ny - d, ny)
         remote(wall.at[piece], wall.at[piece], wf_send.at[d], wf_recv.at[d], sibling).wait_recv()
@@ -330,6 +360,8 @@
     for dx, dz in col_peers:
         send(remote(nown, ngot.at[dx, dz], n_send.at[dx, dz], n_recv.at[dx, dz], at_xz(dx, dz)))
     coeff_low[...] = coeff_t[...].astype(BF16)
+    basis = dot_nt(left, high) + dot_nt(left, low)
+    basis_low[...] = basis.astype(BF16)
     begin = row * frows
     if cols_dev >= 2 * LANES:
         tile = jnp.minimum(begin // LANES, cols_dev // LANES - 2)
@@ -407,7 +439,7 @@
         sem(ny), sem(ny), sem(ny), sem(ny),
         sem(nx, nz), sem(nx, nz), sem(nz), sem(nz), sem(nz), sem(nz), sem(nx, nz), sem(nx, nz),
         sem(ny, 2), sem(ny, 2), sem(nx, nz), sem(nx, nz), sem(1), sem(1),
-        sem(ny), sem(ny), sem(ny), sem(ny), sem(ny), sem(ny), sem(ny), sem(ny),
+        sem(2), sem(2), sem(ny, 2), sem(ny, 2), sem(ny, 2), sem(ny, 2), sem(ny), sem(ny),
         sem(nx, nz), sem(nx, nz),
     ]
     momentum, gradient, right_factor = [

time: 82.3 us -> 77.3 us (0.939)
  Pallas kernels: 81.5 us -> 76.5 us
    pallas_call x1, Pallas kernels: 79.8 us -> 74.8 us  [body(): pl.pallas_call(functools.partial(step_kernel, (ny, nx, nz, scale)), out_s...]
where the time goes in v4:
time: 77.3 us; the launch traced here: 77.2 us
  Pallas kernels  76.5 us (99%)
    pallas_call x1, Pallas kernels, body(): pl.pallas_call(functools.partial(step_kernel, (ny, nx, nz, scale)), out_s...  74.8 us
    pallas_call x1, Pallas kernels, body(): pl.pallas_call(outputs_kernel, out_shape=[jax.ShapeDtypeStruct((rows_dev,...  1.75 us

profile of v4, /device:TPU:1, one launch (start us, length us, event | category | flops | bytes accessed | tf_op | source)
XLA Modules:
  0.0 77.2 jit_solution(1450123967121156401)
XLA Ops:
  0.6 74.8 %panel_and_factor.1 = (bf16[512,1152]{1,0:T(8,128)(2,1)S(1)}, bf16[512,256]{1,0:T(8,128)(2,1)S(1)}, bf16[512,256]{1,0:T(8,128)(2,1)S(1)}, bf16[256,1152]{1,0:T(8,128)(2,1)S(1)}, f32[72,256]{1,0:T(8,128)S(1)}) custom-call(bf16[512,1152]{1,0:T(8,128)(2,1)} %momentum.1, bf16[512,1152]{1,0:T(8,128)(2,1)} %gradient.1, f32[72,256]{1,0:T(8,128)} %factor.1), custom_call_target="tpu_custom_call" | custom-call | tf_op jit(solution)/shard_map/panel_and_factor/pallas_call | solution.py:450
  75.4 1.8 %momentum_and_update.1 = (bf16[512,1152]{1,0:T(8,128)(2,1)}, bf16[512,1152]{1,0:T(8,128)(2,1)}, f32[72,256]{1,0:T(8,128)}) custom-call(bf16[512,1152]{1,0:T(8,128)(2,1)S(1)} %get-tuple-element.8.buffer, bf16[512,256]{1,0:T(8,128)(2,1)S(1)} %get-tuple-element.9.basis, bf16[512,256]{1,0:T(8,128)(2,1)S(1)} %get-tuple-element.10.scaled, ...), custom_call_target="tpu_custom_call" | custom-call | tf_op jit(solution)/shard_map/momentum_and_update/pallas_call | solution.py:468

commit v5 on v4

--- a/solution.py
+++ b/solution.py
@@ -32,14 +32,14 @@
     return jnp.broadcast_to(rows[:, lane : lane + 1], (rows.shape[0], LANES))
 
 
-def eliminate(block, hook=None):
+def eliminate(block, hooks):
     n = LANES
     lanes = lax.broadcasted_iota(jnp.int32, (8, LANES), 1)
     sublane = lax.broadcasted_iota(jnp.int32, (8, LANES), 0)
     groups = [block[8 * g : 8 * g + 8, :] for g in range(n // 8)]
     for j in range(n // 8):
-        if hook is not None and j == n // 16:
-            hook()
+        if j in hooks:
+            hooks[j]()
         base = 8 * j
         inside = (lanes >= base) & (lanes < base + 8)
         rows = [jnp.broadcast_to(groups[j][k : k + 1, :], (8, LANES)) for k in range(8)]
@@ -95,16 +95,16 @@
     return product(a_high, b_high) + (product(a_high, b_low) + product(a_low, b_high))
 
 
-def inverse_lower(work, out_ref, hook):
-    top, rest = slice(0, LANES), slice(LANES, 2 * LANES)
-    first = eliminate(work[top, top])
+def inverse_lower(leading, rest, out_ref, early, late):
+    top, bottom = slice(0, LANES), slice(LANES, 2 * LANES)
+    first = eliminate(leading, {2: early})
     out_ref[top, top] = first
-    out_ref[top, rest] = jnp.zeros((LANES, LANES), F32)
-    upper = exact(first, work[top, rest], (1, 0))
-    schur = work[rest, rest] - exact(upper, upper, (0, 0))
-    second = eliminate(schur, hook)
-    out_ref[rest, rest] = second
-    out_ref[rest, top] = -exact(second, exact(upper, first, (0, 0)), (1, 0))
+    out_ref[top, bottom] = jnp.zeros((LANES, LANES), F32)
+    across, trailing = rest()
+    upper = exact(first, across, (1, 1))
+    second = eliminate(trailing - exact(upper, upper, (0, 0)), {LANES // 16: late})
+    out_ref[bottom, bottom] = second
+    out_ref[bottom, top] = -exact(second, exact(upper, first, (0, 0)), (1, 0))
 
 
 def remote(src, dst, send, recv, device):
@@ -127,8 +127,8 @@
 ):
     ny, nx, nz, scale = sizes
     (
-        grad, fown, fslot, fall, part, psend, xgot, zsend, zgot, panel, panel_t,
-        gpart, ggot, gall, work, lower_inv, wpart, wsib, wsibgot, wsend, wgot, wall, coeff_t,
+        grad, fown, fslot, fall, part, psend, xgot, zsend, zgot, panel,
+        gpart, ggot, gall, lower_inv, wpart, wsib, wsibgot, wsend, wgot, wall, coeff_t,
         nown, ngot,
         local_sem, f_send, f_recv, fs_send, fs_recv,
         x_send, x_recv, z_send, z_recv, pz_send, pz_recv, px_send, px_recv,
@@ -260,15 +260,15 @@
     left = panel[...].reshape(rows_dev, rank)
     left_t = left.T
     halves = rank // 2
-    panel_t[...] = left_t.reshape(2, halves, rows_dev)
 
     grow = rank // ncol
     gram = dot(left_t, left)
     for h in range(2):
         gpart[h] = gram[:, h * LANES : (h + 1) * LANES].reshape(ncol, grow, LANES)
     gpeers = [(d, flip) for d in range(ny) for flip in range(2) if (d, flip) != (0, 0)]
+    own_half = jnp.where(col < ncol // 2, 0, core)
     for d, flip in gpeers:
-        half = core if flip == 0 else 1 - core
+        half = own_half if flip == 0 else jnp.where(col < ncol // 2, 0, 1 - core)
         send(remote(gpart.at[half, col], ggot.at[d, flip], gy_send.at[d, flip], gy_recv.at[d, flip], at_y(d, flip)))
 
     wrow = halves // ny
@@ -276,17 +276,14 @@
     cuts = [0, (tiles + 1) // 2 * LANES, cols_dev] if tiles > 1 else [0, cols_dev]
     parts = [pl.ds(a, b - a) for a, b in zip(cuts[:-1], cuts[1:])]
     for p, lot in enumerate(parts):
-        value = dot(panel_t[1 - core], buf[:, lot])
-        wsib[:, :, lot] = value.astype(BF16).reshape(ny, wrow, lot.size)
+        wpart[:, :, :, lot] = dot(left_t, buf[:, lot]).reshape(2, ny, wrow, lot.size)
+        wsib[:, :, lot] = wpart[1 - core, :, :, lot].astype(BF16)
         src, dst = wsib.at[:, :, lot], wsibgot.at[:, :, lot]
         send(remote(src, dst, ws_send.at[p], ws_recv.at[p], sibling))
 
-    value = dot(panel_t[core], buf[...])
-    wpart[...] = value.reshape(ny, wrow, cols_dev)
-
     def merged(d, lot):
         piece = lax.rem(y + d, ny)
-        return wpart[piece, :, lot] + wsibgot[piece, :, lot].astype(F32)
+        return wpart[core, piece, :, lot] + wsibgot[piece, :, lot].astype(F32)
 
     def spread(p, lot):
         got = wsibgot.at[:, :, lot]
@@ -310,7 +307,7 @@
             send(remote(block, block, wa_send.at[d, p], wa_recv.at[d, p], at_y(d)))
 
     spread(0, parts[0])
-    value = gpart[core, col]
+    value = gpart[own_half, col]
     for d, flip in gpeers:
         remote(ggot.at[d, flip], ggot.at[d, flip], gy_send.at[d, flip], gy_recv.at[d, flip], at_y(d, flip)).wait_recv()
         value = value + ggot[d, flip]
@@ -325,12 +322,17 @@
     for dx, dz in col_peers[::-1]:
         piece = gall.at[core, col_of(-dx, -dz)]
         remote(piece, piece, gx_send.at[dx, dz], gx_recv.at[dx, dz], at_xz(dx, dz)).wait_recv()
-    send(remote(gall.at[core], gall.at[core], gs_send.at[0], gs_recv.at[0], sibling))
-    finish(len(parts) - 1, parts[-1])
-    send(remote(wall.at[mine], wall.at[mine], wf_send.at[0], wf_recv.at[0], sibling))
-    remote(gall.at[1 - core], gall.at[1 - core], gs_send.at[0], gs_recv.at[0], sibling).wait_recv()
-    for h in range(2):
-        work[:, h * LANES : (h + 1) * LANES] = gall[h].reshape(rank, LANES)
+    lower_rows = pl.ds(ncol // 2, ncol // 2)
+    ours, theirs = gall.at[core, lower_rows], gall.at[1 - core, lower_rows]
+    send(remote(ours, ours, gs_send.at[0], gs_recv.at[0], sibling))
+
+    def rest():
+        remote(theirs, theirs, gs_send.at[0], gs_recv.at[0], sibling).wait_recv()
+        return [gall[h, lower_rows].reshape(LANES, LANES) for h in range(2)]
+
+    def finish_last():
+        finish(len(parts) - 1, parts[-1])
+        send(remote(wall.at[mine], wall.at[mine], wf_send.at[0], wf_recv.at[0], sibling))
 
     def arrive(d):
         piece = core * ny + lax.rem(y + ny - d, ny)
@@ -343,14 +345,16 @@
         for d in near:
             arrive(d)
 
-    inverse_lower(work, lower_inv, forward)
+    leading = gall[core, pl.ds(0, ncol // 2)].reshape(LANES, LANES)
+    inverse_lower(leading, rest, lower_inv, finish_last, forward)
     high, low = split(lower_inv[...])
     for d in range(ny):
         piece = (1 - core) * ny + lax.rem(y + ny - d, ny)
         remote(wall.at[piece], wall.at[piece], wf_send.at[d], wf_recv.at[d], sibling).wait_recv()
 
     together = wall[...].reshape(rank, cols_dev)
-    coeff_t[...] = dot(high, together) + dot(low, together)
+    both = dot(jnp.concatenate([high, low], axis=0), together)
+    coeff_t[...] = both[:rank] + both[rank:]
     squares = jnp.zeros((rank, LANES), F32)
     for i in range(cols_dev // LANES):
         value = coeff_t[:, i * LANES : (i + 1) * LANES]
@@ -420,13 +424,11 @@
         pltpu.VMEM((nz, prow, rank), BF16),
         pltpu.VMEM((nz, prow, rank), BF16),
         pltpu.VMEM((ncol, prow, rank), BF16),
-        pltpu.VMEM((2, rank // 2, rows_dev), BF16),
         pltpu.VMEM((2, ncol, grow, LANES), F32),
         pltpu.VMEM((ny, 2, grow, LANES), F32),
         pltpu.VMEM((2, ncol, grow, LANES), F32),
         pltpu.VMEM((rank, rank), F32),
-        pltpu.VMEM((rank, rank), F32),
-        pltpu.VMEM((ny, wrow, cols_dev), F32),
+        pltpu.VMEM((2, ny, wrow, cols_dev), F32),
         pltpu.VMEM((ny, wrow, cols_dev), BF16),
         pltpu.VMEM((ny, wrow, cols_dev), BF16),
         pltpu.VMEM((ny, wrow, cols_dev), BF16),

time: 77.3 us -> 81.5 us (1.054)
  Pallas kernels: 76.5 us -> 80.7 us
    pallas_call x1, Pallas kernels: 74.8 us -> 79 us  [body(): pl.pallas_call(functools.partial(step_kernel, (ny, nx, nz, scale)), out_s...]
where the time goes in v5:
time: 81.5 us; the launch traced here: 81.4 us
  Pallas kernels  80.7 us (99%)
    pallas_call x1, Pallas kernels, body(): pl.pallas_call(functools.partial(step_kernel, (ny, nx, nz, scale)), out_s...  79 us
    pallas_call x1, Pallas kernels, body(): pl.pallas_call(outputs_kernel, out_shape=[jax.ShapeDtypeStruct((rows_dev,...  1.75 us

profile of v5, /device:TPU:1, one launch (start us, length us, event | category | flops | bytes accessed | tf_op | source)
XLA Modules:
  0.0 81.4 jit_solution(9958836536192358998)
XLA Ops:
  0.6 79.0 %panel_and_factor.1 = (bf16[512,1152]{1,0:T(8,128)(2,1)S(1)}, bf16[512,256]{1,0:T(8,128)(2,1)S(1)}, bf16[512,256]{1,0:T(8,128)(2,1)S(1)}, bf16[256,1152]{1,0:T(8,128)(2,1)S(1)}, f32[72,256]{1,0:T(8,128)S(1)}) custom-call(bf16[512,1152]{1,0:T(8,128)(2,1)} %momentum.1, bf16[512,1152]{1,0:T(8,128)(2,1)} %gradient.1, f32[72,256]{1,0:T(8,128)} %factor.1), custom_call_target="tpu_custom_call" | custom-call | tf_op jit(solution)/shard_map/panel_and_factor/pallas_call | solution.py:452
  79.6 1.8 %momentum_and_update.1 = (bf16[512,1152]{1,0:T(8,128)(2,1)}, bf16[512,1152]{1,0:T(8,128)(2,1)}, f32[72,256]{1,0:T(8,128)}) custom-call(bf16[512,1152]{1,0:T(8,128)(2,1)S(1)} %get-tuple-element.8.buffer, bf16[512,256]{1,0:T(8,128)(2,1)S(1)} %get-tuple-element.9.basis, bf16[512,256]{1,0:T(8,128)(2,1)S(1)} %get-tuple-element.10.scaled, ...), custom_call_target="tpu_custom_call" | custom-call | tf_op jit(solution)/shard_map/momentum_and_update/pallas_call | solution.py:470

commit v6 on v5

--- a/solution.py
+++ b/solution.py
@@ -127,7 +127,7 @@
 ):
     ny, nx, nz, scale = sizes
     (
-        grad, fown, fslot, fall, part, psend, xgot, zsend, zgot, panel,
+        grad, fown, fslot, fall, part, psend, xgot, zsend, zgot, panel, panel_t,
         gpart, ggot, gall, lower_inv, wpart, wsib, wsibgot, wsend, wgot, wall, coeff_t,
         nown, ngot,
         local_sem, f_send, f_recv, fs_send, fs_recv,
@@ -260,6 +260,7 @@
     left = panel[...].reshape(rows_dev, rank)
     left_t = left.T
     halves = rank // 2
+    panel_t[...] = left_t.reshape(2, halves, rows_dev)
 
     grow = rank // ncol
     gram = dot(left_t, left)
@@ -276,14 +277,17 @@
     cuts = [0, (tiles + 1) // 2 * LANES, cols_dev] if tiles > 1 else [0, cols_dev]
     parts = [pl.ds(a, b - a) for a, b in zip(cuts[:-1], cuts[1:])]
     for p, lot in enumerate(parts):
-        wpart[:, :, :, lot] = dot(left_t, buf[:, lot]).reshape(2, ny, wrow, lot.size)
-        wsib[:, :, lot] = wpart[1 - core, :, :, lot].astype(BF16)
+        value = dot(panel_t[1 - core], buf[:, lot])
+        wsib[:, :, lot] = value.astype(BF16).reshape(ny, wrow, lot.size)
         src, dst = wsib.at[:, :, lot], wsibgot.at[:, :, lot]
         send(remote(src, dst, ws_send.at[p], ws_recv.at[p], sibling))
 
+    value = dot(panel_t[core], buf[...])
+    wpart[...] = value.reshape(ny, wrow, cols_dev)
+
     def merged(d, lot):
         piece = lax.rem(y + d, ny)
-        return wpart[core, piece, :, lot] + wsibgot[piece, :, lot].astype(F32)
+        return wpart[piece, :, lot] + wsibgot[piece, :, lot].astype(F32)
 
     def spread(p, lot):
         got = wsibgot.at[:, :, lot]
@@ -353,8 +357,7 @@
         remote(wall.at[piece], wall.at[piece], wf_send.at[d], wf_recv.at[d], sibling).wait_recv()
 
     together = wall[...].reshape(rank, cols_dev)
-    both = dot(jnp.concatenate([high, low], axis=0), together)
-    coeff_t[...] = both[:rank] + both[rank:]
+    coeff_t[...] = dot(high, together) + dot(low, together)
     squares = jnp.zeros((rank, LANES), F32)
     for i in range(cols_dev // LANES):
         value = coeff_t[:, i * LANES : (i + 1) * LANES]
@@ -424,11 +427,12 @@
         pltpu.VMEM((nz, prow, rank), BF16),
         pltpu.VMEM((nz, prow, rank), BF16),
         pltpu.VMEM((ncol, prow, rank), BF16),
+        pltpu.VMEM((2, rank // 2, rows_dev), BF16),
         pltpu.VMEM((2, ncol, grow, LANES), F32),
         pltpu.VMEM((ny, 2, grow, LANES), F32),
         pltpu.VMEM((2, ncol, grow, LANES), F32),
         pltpu.VMEM((rank, rank), F32),
-        pltpu.VMEM((2, ny, wrow, cols_dev), F32),
+        pltpu.VMEM((ny, wrow, cols_dev), F32),
         pltpu.VMEM((ny, wrow, cols_dev), BF16),
         pltpu.VMEM((ny, wrow, cols_dev), BF16),
         pltpu.VMEM((ny, wrow, cols_dev), BF16),

time: 81.5 us -> 81.5 us (level)
  no operation moved by 1% of the time
where the time goes in v6:
time: 81.5 us; the launch traced here: 81.3 us
  Pallas kernels  80.7 us (99%)
    pallas_call x1, Pallas kernels, body(): pl.pallas_call(functools.partial(step_kernel, (ny, nx, nz, scale)), out_s...  78.9 us
    pallas_call x1, Pallas kernels, body(): pl.pallas_call(outputs_kernel, out_shape=[jax.ShapeDtypeStruct((rows_dev,...  1.75 us

profile of v6, /device:TPU:1, one launch (start us, length us, event | category | flops | bytes accessed | tf_op | source)
XLA Modules:
  0.0 81.3 jit_solution(11281981998709919690)
XLA Ops:
  0.6 78.9 %panel_and_factor.1 = (bf16[512,1152]{1,0:T(8,128)(2,1)S(1)}, bf16[512,256]{1,0:T(8,128)(2,1)S(1)}, bf16[512,256]{1,0:T(8,128)(2,1)S(1)}, bf16[256,1152]{1,0:T(8,128)(2,1)S(1)}, f32[72,256]{1,0:T(8,128)S(1)}) custom-call(bf16[512,1152]{1,0:T(8,128)(2,1)} %momentum.1, bf16[512,1152]{1,0:T(8,128)(2,1)} %gradient.1, f32[72,256]{1,0:T(8,128)} %factor.1), custom_call_target="tpu_custom_call" | custom-call | tf_op jit(solution)/shard_map/panel_and_factor/pallas_call | solution.py:456
  79.6 1.8 %momentum_and_update.1 = (bf16[512,1152]{1,0:T(8,128)(2,1)}, bf16[512,1152]{1,0:T(8,128)(2,1)}, f32[72,256]{1,0:T(8,128)}) custom-call(bf16[512,1152]{1,0:T(8,128)(2,1)S(1)} %get-tuple-element.8.buffer, bf16[512,256]{1,0:T(8,128)(2,1)S(1)} %get-tuple-element.9.basis, bf16[512,256]{1,0:T(8,128)(2,1)S(1)} %get-tuple-element.10.scaled, ...), custom_call_target="tpu_custom_call" | custom-call | tf_op jit(solution)/shard_map/momentum_and_update/pallas_call | solution.py:474

commit v7 on v4

--- a/solution.py
+++ b/solution.py
@@ -127,11 +127,11 @@
 ):
     ny, nx, nz, scale = sizes
     (
-        grad, fown, fslot, fall, part, psend, xgot, zsend, zgot, panel, panel_t,
+        grad, fown, fslot, fall, part, psend, xgot, panel, panel_t,
         gpart, ggot, gall, work, lower_inv, wpart, wsib, wsibgot, wsend, wgot, wall, coeff_t,
         nown, ngot,
         local_sem, f_send, f_recv, fs_send, fs_recv,
-        x_send, x_recv, z_send, z_recv, pz_send, pz_recv, px_send, px_recv,
+        x_send, x_recv, px_send, px_recv,
         gy_send, gy_recv, gx_send, gx_recv, gs_send, gs_recv,
         ws_send, ws_recv, wy_send, wy_recv, wa_send, wa_recv, wf_send, wf_recv,
         n_send, n_recv,
@@ -221,41 +221,28 @@
     prow = rows_dev // ncol
     right = fall[...].astype(BF16)
     many = rows_dev // nx
-    order = sorted(range(1, nz), key=lambda d: -min(d, nz - d)) + [0]
-    for dx in list(range(1, nx)) + [0]:
+    for dx in sorted(range(nx), key=lambda d: -min(d, nx - d)):
         group = lax.rem(x + dx, nx)
         value = dot(buf[pl.ds(pl.multiple_of(group * many, many), many), :], right).reshape(nz, prow, rank)
         if dx == 0:
             part[...] = value
-            continue
         psend[dx] = value.astype(BF16)
-        for dz in order:
-            src = psend.at[dx, lax.rem(z + dz, nz)]
-            send(remote(src, xgot.at[dx, dz], x_send.at[dx, dz], x_recv.at[dx, dz], at_x(dx)))
-    for dz in order:
-        value = part[lax.rem(z + dz, nz)]
-        for dx in range(1, nx):
-            remote(xgot.at[dx, dz], xgot.at[dx, dz], x_send.at[dx, dz], x_recv.at[dx, dz], at_x(dx)).wait_recv()
-            value = value + xgot[dx, dz].astype(F32)
-        if dz:
-            zsend[dz] = value.astype(BF16)
-            send(remote(zsend.at[dz], zgot.at[dz], z_send.at[dz], z_recv.at[dz], at_z(dz)))
-    for dz in sorted(range(1, nz), key=lambda d: min(d, nz - d)):
-        remote(zgot.at[dz], zgot.at[dz], z_send.at[dz], z_recv.at[dz], at_z(dz)).wait_recv()
-        value = value + zgot[dz].astype(F32)
+        for dz in sorted(range(nz), key=lambda d: -min(d, nz - d)):
+            if (dx, dz) != (0, 0):
+                src, dst = psend.at[dx, lax.rem(z + dz, nz)], xgot.at[dx, dz]
+                send(remote(src, dst, x_send.at[dx, dz], x_recv.at[dx, dz], at_xz(dx, dz)))
+    value = part[z]
+    for dx, dz in col_peers[::-1]:
+        got = xgot.at[dx, dz]
+        remote(got, got, x_send.at[dx, dz], x_recv.at[dx, dz], at_xz(dx, dz)).wait_recv()
+        value = value + xgot[dx, dz].astype(F32)
     panel[col] = value.astype(BF16)
-    for dz in order[:-1]:
-        send(remote(panel.at[col], panel.at[col], pz_send.at[dz], pz_recv.at[dz], at_z(dz)))
-    for dz in [0] + sorted(range(1, nz), key=lambda d: min(d, nz - d)):
-        piece = x * nz + lax.rem(z + nz - dz, nz)
-        if dz:
-            remote(panel.at[piece], panel.at[piece], pz_send.at[dz], pz_recv.at[dz], at_z(dz)).wait_recv()
-        for dx in range(1, nx):
-            send(remote(panel.at[piece], panel.at[piece], px_send.at[dx, dz], px_recv.at[dx, dz], at_x(dx)))
-    for dz in range(nz):
-        for dx in range(1, nx):
-            piece = lax.rem(x + nx - dx, nx) * nz + lax.rem(z + nz - dz, nz)
-            remote(panel.at[piece], panel.at[piece], px_send.at[dx, dz], px_recv.at[dx, dz], at_x(dx)).wait_recv()
+    for dx, dz in col_peers:
+        block = panel.at[col]
+        send(remote(block, block, px_send.at[dx, dz], px_recv.at[dx, dz], at_xz(dx, dz)))
+    for dx, dz in col_peers[::-1]:
+        block = panel.at[col_of(-dx, -dz)]
+        remote(block, block, px_send.at[dx, dz], px_recv.at[dx, dz], at_xz(dx, dz)).wait_recv()
 
     left = panel[...].reshape(rows_dev, rank)
     left_t = left.T
@@ -417,8 +404,6 @@
         pltpu.VMEM((nz, prow, rank), F32),
         pltpu.VMEM((nx, nz, prow, rank), BF16),
         pltpu.VMEM((nx, nz, prow, rank), BF16),
-        pltpu.VMEM((nz, prow, rank), BF16),
-        pltpu.VMEM((nz, prow, rank), BF16),
         pltpu.VMEM((ncol, prow, rank), BF16),
         pltpu.VMEM((2, rank // 2, rows_dev), BF16),
         pltpu.VMEM((2, ncol, grow, LANES), F32),
@@ -437,7 +422,7 @@
         pltpu.VMEM((nx, nz, 1, rank), F32),
         sem(3),
         sem(ny), sem(ny), sem(ny), sem(ny),
-        sem(nx, nz), sem(nx, nz), sem(nz), sem(nz), sem(nz), sem(nz), sem(nx, nz), sem(nx, nz),
+        sem(nx, nz), sem(nx, nz), sem(nx, nz), sem(nx, nz),
         sem(ny, 2), sem(ny, 2), sem(nx, nz), sem(nx, nz), sem(1), sem(1),
         sem(2), sem(2), sem(ny, 2), sem(ny, 2), sem(ny, 2), sem(ny, 2), sem(ny), sem(ny),
         sem(nx, nz), sem(nx, nz),

time: 77.3 us -> 77.1 us (level)
  no operation moved by 1% of the time
where the time goes in v7:
time: 77.1 us; the launch traced here: 76.9 us
  Pallas kernels  76.3 us (99%)
    pallas_call x1, Pallas kernels, body(): pl.pallas_call(functools.partial(step_kernel, (ny, nx, nz, scale)), out_s...  74.5 us
    pallas_call x1, Pallas kernels, body(): pl.pallas_call(outputs_kernel, out_shape=[jax.ShapeDtypeStruct((rows_dev,...  1.75 us

profile of v7, /device:TPU:1, one launch (start us, length us, event | category | flops | bytes accessed | tf_op | source)
XLA Modules:
  0.0 76.9 jit_solution(14404193678430789332)
XLA Ops:
  0.6 74.5 %panel_and_factor.1 = (bf16[512,1152]{1,0:T(8,128)(2,1)S(1)}, bf16[512,256]{1,0:T(8,128)(2,1)S(1)}, bf16[512,256]{1,0:T(8,128)(2,1)S(1)}, bf16[256,1152]{1,0:T(8,128)(2,1)S(1)}, f32[72,256]{1,0:T(8,128)S(1)}) custom-call(bf16[512,1152]{1,0:T(8,128)(2,1)} %momentum.1, bf16[512,1152]{1,0:T(8,128)(2,1)} %gradient.1, f32[72,256]{1,0:T(8,128)} %factor.1), custom_call_target="tpu_custom_call" | custom-call | tf_op jit(solution)/shard_map/panel_and_factor/pallas_call | solution.py:435
  75.2 1.7 %momentum_and_update.1 = (bf16[512,1152]{1,0:T(8,128)(2,1)}, bf16[512,1152]{1,0:T(8,128)(2,1)}, f32[72,256]{1,0:T(8,128)}) custom-call(bf16[512,1152]{1,0:T(8,128)(2,1)S(1)} %get-tuple-element.8.buffer, bf16[512,256]{1,0:T(8,128)(2,1)S(1)} %get-tuple-element.9.basis, bf16[512,256]{1,0:T(8,128)(2,1)S(1)} %get-tuple-element.10.scaled, ...), custom_call_target="tpu_custom_call" | custom-call | tf_op jit(solution)/shard_map/momentum_and_update/pallas_call | solution.py:453
